TPU v7x, 32 devices: a whole 2x2x4 slice. The times are simulated.
32 devices in a mesh: seq: 16 (over z, x, core), head: 2 (over y).
Axes of the slice: x: 2, y: 2, z: 4, core: 2. Of those that a mesh axis runs over, the one named last changes fastest.
Arguments:
- queries: bfloat16 [2048, 8192], P('seq', 'head'), may hold values from -14 to 14, as said below
- key_tokens: bfloat16 [2048, 1024], P(('seq', 'head')), may hold values from -6 to 6, as said below
- value_tokens: bfloat16 [2048, 1024], P(('seq', 'head')), may hold values from -6 to 6
- key_scales: bfloat16 [32, 8], P('seq', 'head'), may hold values from 0.25 to 2.5
- value_scales: bfloat16 [32, 8], P('seq', 'head'), may hold values from 0.25 to 2.5
- value_means: float32 [1024], P('head'), may hold values from -4 to 4
- doc_lengths: int32 [64], replicated, may hold values from 1 to 1280, 2048 in all
Outputs:
- attended: bfloat16 [2048, 8192], P('seq', 'head')
Inputs may be any that keep to these rules, and one draw needn't show every extreme that they name: `doc_lengths`: positive lengths of the documents in order; they sum to 2048, and the longest has exactly 1280 tokens. `queries`: finite values. `key_tokens`: finite values.
All inputs are finite; a program needn't handle non-finite values.
Results may differ from a plain program's by a relative error of at most 0.002.
Values may be sent and summed in bfloat16 or wider, within the bound.
A program may use at most 64 MiB of HBM per device.

v0:
```python
import math

import jax
import jax.numpy as jnp
from jax import lax
from jax.sharding import PartitionSpec as P

QH = 64
KVH = 8
HD = 128
BLK = 64


NEG = -1e30


def doc_index(positions, starts):
    return jnp.sum((starts[None, :] <= positions[:, None]).astype(jnp.int32), axis=1) - 1


def block_update(
    totals,
    query_tile,
    query_pos,
    query_doc,
    key_tile,
    value_tile,
    key_scale,
    value_scale,
    key_pos,
    starts,
):
    inv_scale = 1.0 / math.sqrt(HD)
    key_doc = doc_index(key_pos, starts)
    allowed = (key_doc[None, :] == query_doc[:, None]) & (key_pos[None, :] <= query_pos[:, None])

    def update(current):
        run_max, run_sum, accumulate = current
        scores = jnp.einsum(
            "kgrd,nkd->kgrn", query_tile, key_tile, preferred_element_type=jnp.float32
        )
        scores = scores * (key_scale.T * inv_scale)[:, None, None, :]
        scores = jnp.where(allowed[None, None], scores, NEG)
        new_max = jnp.maximum(run_max, jnp.max(scores, axis=-1))
        weights = jnp.where(allowed[None, None], jnp.exp(scores - new_max[..., None]), 0.0)
        factor = jnp.exp(run_max - new_max)
        run_sum = run_sum * factor + jnp.sum(weights, axis=-1)
        scaled = (weights * value_scale.T[:, None, None, :]).astype(jnp.bfloat16)
        accumulate = accumulate * factor[..., None] + jnp.einsum(
            "kgrn,nkd->kgrd", scaled, value_tile, preferred_element_type=jnp.float32
        )
        return (new_max, run_sum, accumulate)

    def keep_state(current):
        return current

    return lax.cond(jnp.any(allowed), update, keep_state, totals)


def fold_packet(totals, packet, query_tile, query_pos, query_doc, starts, heads_kv):
    block_count = packet.shape[0]
    sub_blocks = math.gcd(block_count, max(1, 256 // BLK))
    step_count = block_count // sub_blocks
    key_count = sub_blocks * BLK
    key_part = packet[:, 0, :BLK, :].reshape(step_count, key_count, heads_kv, HD)
    value_part = packet[:, 1, :BLK, :].reshape(step_count, key_count, heads_kv, HD)
    key_scale = packet[:, 0, BLK, :].reshape(block_count, heads_kv, HD)[:, :, 0].astype(jnp.float32)
    value_scale = (
        packet[:, 1, BLK, :].reshape(block_count, heads_kv, HD)[:, :, 0].astype(jnp.float32)
    )
    key_scale = jnp.repeat(key_scale, BLK, axis=0).reshape(step_count, key_count, heads_kv)
    value_scale = jnp.repeat(value_scale, BLK, axis=0).reshape(step_count, key_count, heads_kv)
    offsets = jnp.arange(step_count, dtype=jnp.int32) * key_count

    def one_step(current, scan_item):
        key_tile, value_tile, key_sc, value_sc, offset = scan_item
        key_pos = offset + jnp.arange(key_count, dtype=jnp.int32)
        return (
            block_update(
                current,
                query_tile,
                query_pos,
                query_doc,
                key_tile,
                value_tile,
                key_sc,
                value_sc,
                key_pos,
                starts,
            ),
            None,
        )

    totals, _ = lax.scan(one_step, totals, (key_part, value_part, key_scale, value_scale, offsets))
    return totals


def finish(totals, value_means, heads_kv, group_size, row_count):
    run_max, run_sum, accumulate = totals
    result = accumulate / run_sum[..., None] + value_means.reshape(heads_kv, 1, 1, HD)
    return (
        result.transpose(2, 0, 1, 3)
        .reshape(row_count, heads_kv * group_size * HD)
        .astype(jnp.bfloat16)
    )


def shards(queries, key_tokens, value_tokens, key_scales, value_scales, value_means, doc_lengths):
    local_keys, local_values = (
        lax.all_to_all(key_tokens, "head", split_axis=1, concat_axis=0, tiled=True),
        lax.all_to_all(value_tokens, "head", split_axis=1, concat_axis=0, tiled=True),
    )
    row_count = local_keys.shape[0]
    heads_kv = local_keys.shape[1] // HD
    group_size = QH // KVH
    blocks = row_count // BLK
    seq_index = lax.axis_index("seq")
    starts = jnp.cumsum(doc_lengths) - doc_lengths
    key_rows = jnp.concatenate(
        [
            local_keys.reshape(blocks, BLK, heads_kv * HD),
            jnp.repeat(key_scales, HD, axis=1)[:, None, :],
        ],
        axis=1,
    )
    value_rows = jnp.concatenate(
        [
            local_values.reshape(blocks, BLK, heads_kv * HD),
            jnp.repeat(value_scales, HD, axis=1)[:, None, :],
        ],
        axis=1,
    )
    bundle = jnp.stack([key_rows, value_rows], axis=1)

    def prepare(query_rows, query_pos):
        query_tile = query_rows.reshape(query_rows.shape[0], heads_kv, group_size, HD).transpose(
            1, 2, 0, 3
        )
        query_doc = doc_index(query_pos, starts)
        count_rows = query_rows.shape[0]
        initial = (
            jnp.full((heads_kv, group_size, count_rows), NEG, jnp.float32),
            jnp.zeros((heads_kv, group_size, count_rows), jnp.float32),
            jnp.zeros((heads_kv, group_size, count_rows, HD), jnp.float32),
        )

        def folder(totals, packet, first_block):
            return fold_packet(totals, packet, query_tile, query_pos, query_doc, starts, heads_kv)

        return (folder, initial)

    own_pos = seq_index * row_count + jnp.arange(row_count, dtype=jnp.int32)
    folder, initial = prepare(queries, own_pos)
    totals = folder(initial, lax.all_gather(bundle, "seq", axis=0, tiled=True), jnp.int32(0))
    attended = finish(totals, value_means, heads_kv, group_size, row_count)
    return attended


def solution(mesh):
    in_specs = (
        P("seq", "head"),
        P(("seq", "head"), None),
        P(("seq", "head"), None),
        P("seq", "head"),
        P("seq", "head"),
        P("head"),
        P(),
    )
    out_specs = P("seq", "head")
    return jax.shard_map(shards, mesh=mesh, in_specs=in_specs, out_specs=out_specs, check_vma=False)
```

profile of v0, /device:TPU:25, one launch (start us, length us, event | category | flops | bytes accessed | tf_op | source)
XLA Modules:
  0.0 178.4 jit_solution(17557842106516047412)
XLA Ops:
  6.5 1.5 copy.106
  8.1 3.4 %all-to-all-start = ((bf16[64,2,512]{2,0,1:T(8,128)(2,1)}), bf16[64,2,512]{2,0,1:T(8,128)(2,1)S(1)}, u32[]{:S(2)}, u32[]{:S(2)}) async-start(bf16[64,2,512]{2,0,1:T(8,128)(2,1)} %bitcast.73), calls=%async_computation | async-start | bytes 262144 | tf_op jit(solution)/shard_map/all_to_all | solution.py:110
  12.2 1.6 copy.105
  14.8 3.4 %all-to-all-start.1 = ((bf16[64,2,512]{2,0,1:T(8,128)(2,1)}), bf16[64,2,512]{2,0,1:T(8,128)(2,1)S(1)}, u32[]{:S(2)}, u32[]{:S(2)}) async-start(bf16[64,2,512]{2,0,1:T(8,128)(2,1)} %bitcast.72), calls=%async_computation.1 | async-start | bytes 262144 | tf_op jit(solution)/shard_map/all_to_all | solution.py:111
  18.2 3.2 %all-to-all-done.1 = bf16[64,2,512]{2,0,1:T(8,128)(2,1)S(1)} async-done(((bf16[64,2,512]{2,0,1:T(8,128)(2,1)}), bf16[64,2,512]{2,0,1:T(8,128)(2,1)S(1)}, u32[]{:S(2)}, u32[]{:S(2)}) %all-to-all-start.1) | async-done | bytes 131104 | tf_op jit(solution)/shard_map/all_to_all | solution.py:111
  21.5 1.0 copy.78
  24.2 1.6 copy.79
  26.6 48.4 %all-gather.2.cloned.1.call-done = bf16[32,2,65,512]{3,1,2,0:T(2,128)(2,1)} async-done(((bf16[2,2,65,512]{3,1,2,0:T(2,128)(2,1)}), bf16[32,2,65,512]{3,1,2,0:T(2,128)(2,1)}) %all-gather.2.cloned.1.call-update) | async-done | bytes 4259856 | tf_op jit(solution)/shard_map/all_gather | solution.py:154
  75.0 1.2 slice_reduce_fusion.2
  76.5 21.4 %slice_reduce_fusion = (bf16[32,64,512]{2,1,0:T(8,128)(2,1)}, bf16[32,64,512]{2,1,0:T(8,128)(2,1)}) fusion(bf16[32,2,65,512]{3,1,2,0:T(2,128)(2,1)} %all-gather.2.cloned.1.call-done), kind=kLoop, calls=%fused_computation.32 | loop fusion | bytes 8388608 | tf_op jit(solution)/shard_map/slice | solution.py:66
  97.8 2.5 %reshape_squeeze.12 = bf16[8,256,4,128]{3,2,1,0:T(4,128)(2,1)S(1)} reshape(bf16[32,64,512]{2,1,0:T(8,128)(2,1)} %get-tuple-element.435) | data formatting | bytes 4194304 | tf_op jit(solution)/shard_map/reshape;squeeze | solution.py:65
  100.4 1.9 %copy.82 = bf16[8,256,4,128]{3,1,2,0:T(8,128)(2,1)} copy(bf16[8,256,4,128]{3,2,1,0:T(4,128)(2,1)S(1)} %reshape_squeeze.12) | data formatting | bytes 4194304
  102.3 2.5 %reshape_squeeze.15 = bf16[8,256,4,128]{3,2,1,0:T(4,128)(2,1)S(1)} reshape(bf16[32,64,512]{2,1,0:T(8,128)(2,1)} %get-tuple-element.434) | data formatting | bytes 4194304 | tf_op jit(solution)/shard_map/reshape;squeeze | solution.py:66
  104.8 1.8 %copy.84 = bf16[8,256,4,128]{3,1,2,0:T(8,128)(2,1)} copy(bf16[8,256,4,128]{3,2,1,0:T(4,128)(2,1)S(1)} %reshape_squeeze.15) | data formatting | bytes 4194304
  106.9 61.8 %while.17 = (s32[]{:T(128)}, f32[4,8,128]{2,1,0:T(8,128)S(1)}, f32[4,8,128]{2,1,0:T(8,128)S(1)}, f32[4,8,128,128]{3,2,1,0:T(8,128)S(1)}, s32[64]{0:T(128)S(1)}, ...) while((s32[]{:T(128)}, f32[4,8,128]{2,1,0:T(8,128)S(1)}, ...), condition=%wide.region_9.10_spmd.clone, body=%wide.region_2.9_spmd.clone.sunk | while | flops 552789376 | bytes 19000364 | solution.py:94
  108.3 0.8 fusion.24
  111.1 0.8 fusion.24
  112.5 6.6 %conditional.3 = ((f32[4,8,128]{2,1,0:T(8,128)S(1)}, f32[4,8,128]{2,1,0:T(8,128)S(1)}, f32[4,8,128,128]{3,2,1,0:T(8,128)S(1)})) conditional(s32[]{:T(128)} %convert_element_type.65, (f32[4,8,128]{2,1,0:T(8,128)S(1)}, f32[4,8,128]{2,1,0:T(8,128)S(1)}, f32[4,8,128,128]{3,2,1,0:T(8,128)S(1)}) %tuple.65, (pred[128,256]{0,1:T(8,128)(4,1)S(1)}, ...), branch_computations={%region_5.5_spmd, %region_6.8_spmd} | conditional | flops 552608768 | bytes 18958372 | solution.py:57
  112.9 1.7 fusion.6
  114.6 1.1 fusion.7
  115.8 3.3 %multiply_add_fusion = f32[4,8,128,128]{3,2,1,0:T(8,128)S(1)} fusion(f32[4,8,128,128]{3,2,1,0:T(8,128)S(1)} %get-tuple-element.253, f32[4,256,8,128]{3,1,2,0:T(8,128)S(1)} %get-tuple-element.467, f32[4,256]{1,0:T(4,128)S(1)} %bitcast.86, f32[4,8,128]{2,1,0:T(8,128)S(1)} %max.4, f32[4,256]{1,0:T(4,128)S(1)} %fusion.15, ...), kind=kOutput, calls=%fused_computation.8 | convolution fusion | flops 275775488 | bytes 8724992 | tf_op jit(solution)/shard_map/while/body/eval_jaxpr/cond/branch_1_fun/kgrn,nkd->kgrd/dot_general | solution.py:49
  120.5 0.8 fusion.24
  121.9 6.6 %conditional.3 = ((f32[4,8,128]{2,1,0:T(8,128)S(1)}, f32[4,8,128]{2,1,0:T(8,128)S(1)}, f32[4,8,128,128]{3,2,1,0:T(8,128)S(1)})) conditional(s32[]{:T(128)} %convert_element_type.65, (f32[4,8,128]{2,1,0:T(8,128)S(1)}, f32[4,8,128]{2,1,0:T(8,128)S(1)}, f32[4,8,128,128]{3,2,1,0:T(8,128)S(1)}) %tuple.65, (pred[128,256]{0,1:T(8,128)(4,1)S(1)}, ...), branch_computations={%region_5.5_spmd, %region_6.8_spmd} | conditional | flops 552608768 | bytes 18958372 | solution.py:57
  122.3 1.7 fusion.6
  124.0 1.1 fusion.7
  125.1 3.3 %multiply_add_fusion = f32[4,8,128,128]{3,2,1,0:T(8,128)S(1)} fusion(f32[4,8,128,128]{3,2,1,0:T(8,128)S(1)} %get-tuple-element.253, f32[4,256,8,128]{3,1,2,0:T(8,128)S(1)} %get-tuple-element.467, f32[4,256]{1,0:T(4,128)S(1)} %bitcast.86, f32[4,8,128]{2,1,0:T(8,128)S(1)} %max.4, f32[4,256]{1,0:T(4,128)S(1)} %fusion.15, ...), kind=kOutput, calls=%fused_computation.8 | convolution fusion | flops 275775488 | bytes 8724992 | tf_op jit(solution)/shard_map/while/body/eval_jaxpr/cond/branch_1_fun/kgrn,nkd->kgrd/dot_general | solution.py:49
  129.8 0.8 fusion.24
  131.2 6.6 %conditional.3 = ((f32[4,8,128]{2,1,0:T(8,128)S(1)}, f32[4,8,128]{2,1,0:T(8,128)S(1)}, f32[4,8,128,128]{3,2,1,0:T(8,128)S(1)})) conditional(s32[]{:T(128)} %convert_element_type.65, (f32[4,8,128]{2,1,0:T(8,128)S(1)}, f32[4,8,128]{2,1,0:T(8,128)S(1)}, f32[4,8,128,128]{3,2,1,0:T(8,128)S(1)}) %tuple.65, (pred[128,256]{0,1:T(8,128)(4,1)S(1)}, ...), branch_computations={%region_5.5_spmd, %region_6.8_spmd} | conditional | flops 552608768 | bytes 18958372 | solution.py:57
  131.6 1.7 fusion.6
  133.3 1.1 fusion.7
  134.5 3.3 %multiply_add_fusion = f32[4,8,128,128]{3,2,1,0:T(8,128)S(1)} fusion(f32[4,8,128,128]{3,2,1,0:T(8,128)S(1)} %get-tuple-element.253, f32[4,256,8,128]{3,1,2,0:T(8,128)S(1)} %get-tuple-element.467, f32[4,256]{1,0:T(4,128)S(1)} %bitcast.86, f32[4,8,128]{2,1,0:T(8,128)S(1)} %max.4, f32[4,256]{1,0:T(4,128)S(1)} %fusion.15, ...), kind=kOutput, calls=%fused_computation.8 | convolution fusion | flops 275775488 | bytes 8724992 | tf_op jit(solution)/shard_map/while/body/eval_jaxpr/cond/branch_1_fun/kgrn,nkd->kgrd/dot_general | solution.py:49
  139.2 0.8 fusion.24
  140.6 6.6 %conditional.3 = ((f32[4,8,128]{2,1,0:T(8,128)S(1)}, f32[4,8,128]{2,1,0:T(8,128)S(1)}, f32[4,8,128,128]{3,2,1,0:T(8,128)S(1)})) conditional(s32[]{:T(128)} %convert_element_type.65, (f32[4,8,128]{2,1,0:T(8,128)S(1)}, f32[4,8,128]{2,1,0:T(8,128)S(1)}, f32[4,8,128,128]{3,2,1,0:T(8,128)S(1)}) %tuple.65, (pred[128,256]{0,1:T(8,128)(4,1)S(1)}, ...), branch_computations={%region_5.5_spmd, %region_6.8_spmd} | conditional | flops 552608768 | bytes 18958372 | solution.py:57
  141.0 1.7 fusion.6
  142.7 1.1 fusion.7
  143.9 3.3 %multiply_add_fusion = f32[4,8,128,128]{3,2,1,0:T(8,128)S(1)} fusion(f32[4,8,128,128]{3,2,1,0:T(8,128)S(1)} %get-tuple-element.253, f32[4,256,8,128]{3,1,2,0:T(8,128)S(1)} %get-tuple-element.467, f32[4,256]{1,0:T(4,128)S(1)} %bitcast.86, f32[4,8,128]{2,1,0:T(8,128)S(1)} %max.4, f32[4,256]{1,0:T(4,128)S(1)} %fusion.15, ...), kind=kOutput, calls=%fused_computation.8 | convolution fusion | flops 275775488 | bytes 8724992 | tf_op jit(solution)/shard_map/while/body/eval_jaxpr/cond/branch_1_fun/kgrn,nkd->kgrd/dot_general | solution.py:49
  148.5 0.8 fusion.24
  150.0 6.6 %conditional.3 = ((f32[4,8,128]{2,1,0:T(8,128)S(1)}, f32[4,8,128]{2,1,0:T(8,128)S(1)}, f32[4,8,128,128]{3,2,1,0:T(8,128)S(1)})) conditional(s32[]{:T(128)} %convert_element_type.65, (f32[4,8,128]{2,1,0:T(8,128)S(1)}, f32[4,8,128]{2,1,0:T(8,128)S(1)}, f32[4,8,128,128]{3,2,1,0:T(8,128)S(1)}) %tuple.65, (pred[128,256]{0,1:T(8,128)(4,1)S(1)}, ...), branch_computations={%region_5.5_spmd, %region_6.8_spmd} | conditional | flops 552608768 | bytes 18958372 | solution.py:57
  150.3 1.7 fusion.6
  152.1 1.1 fusion.7
  153.2 3.3 %multiply_add_fusion = f32[4,8,128,128]{3,2,1,0:T(8,128)S(1)} fusion(f32[4,8,128,128]{3,2,1,0:T(8,128)S(1)} %get-tuple-element.253, f32[4,256,8,128]{3,1,2,0:T(8,128)S(1)} %get-tuple-element.467, f32[4,256]{1,0:T(4,128)S(1)} %bitcast.86, f32[4,8,128]{2,1,0:T(8,128)S(1)} %max.4, f32[4,256]{1,0:T(4,128)S(1)} %fusion.15, ...), kind=kOutput, calls=%fused_computation.8 | convolution fusion | flops 275775488 | bytes 8724992 | tf_op jit(solution)/shard_map/while/body/eval_jaxpr/cond/branch_1_fun/kgrn,nkd->kgrd/dot_general | solution.py:49
  157.9 0.8 fusion.24
  159.3 6.6 %conditional.3 = ((f32[4,8,128]{2,1,0:T(8,128)S(1)}, f32[4,8,128]{2,1,0:T(8,128)S(1)}, f32[4,8,128,128]{3,2,1,0:T(8,128)S(1)})) conditional(s32[]{:T(128)} %convert_element_type.65, (f32[4,8,128]{2,1,0:T(8,128)S(1)}, f32[4,8,128]{2,1,0:T(8,128)S(1)}, f32[4,8,128,128]{3,2,1,0:T(8,128)S(1)}) %tuple.65, (pred[128,256]{0,1:T(8,128)(4,1)S(1)}, ...), branch_computations={%region_5.5_spmd, %region_6.8_spmd} | conditional | flops 552608768 | bytes 18958372 | solution.py:57
  159.7 1.7 fusion.6
  161.4 1.1 fusion.7
  162.6 3.3 %multiply_add_fusion = f32[4,8,128,128]{3,2,1,0:T(8,128)S(1)} fusion(f32[4,8,128,128]{3,2,1,0:T(8,128)S(1)} %get-tuple-element.253, f32[4,256,8,128]{3,1,2,0:T(8,128)S(1)} %get-tuple-element.467, f32[4,256]{1,0:T(4,128)S(1)} %bitcast.86, f32[4,8,128]{2,1,0:T(8,128)S(1)} %max.4, f32[4,256]{1,0:T(4,128)S(1)} %fusion.15, ...), kind=kOutput, calls=%fused_computation.8 | convolution fusion | flops 275775488 | bytes 8724992 | tf_op jit(solution)/shard_map/while/body/eval_jaxpr/cond/branch_1_fun/kgrn,nkd->kgrd/dot_general | solution.py:49
  167.3 0.8 fusion.24
  170.2 1.4 copy.104
  (133 shorter events, 19.1 us)
Async XLA Ops:
  8.1 6.7 %all-to-all-start = ((bf16[64,2,512]{2,0,1:T(8,128)(2,1)}), bf16[64,2,512]{2,0,1:T(8,128)(2,1)S(1)}, u32[]{:S(2)}, u32[]{:S(2)}) async-start(bf16[64,2,512]{2,0,1:T(8,128)(2,1)} %bitcast.73), calls=%async_computation | async-start | bytes 262144 | tf_op jit(solution)/shard_map/all_to_all | solution.py:110
  14.8 6.7 %all-to-all-start.1 = ((bf16[64,2,512]{2,0,1:T(8,128)(2,1)}), bf16[64,2,512]{2,0,1:T(8,128)(2,1)S(1)}, u32[]{:S(2)}, u32[]{:S(2)}) async-start(bf16[64,2,512]{2,0,1:T(8,128)(2,1)} %bitcast.72), calls=%async_computation.1 | async-start | bytes 262144 | tf_op jit(solution)/shard_map/all_to_all | solution.py:111
  18.2 56.8 %all-gather.2.cloned.1.call-start = ((), (), s32[]{:S(2)}) async-start(), calls=%async_computation.2 | async-start | bytes 4526080 | tf_op jit(solution)/shard_map/all_gather | solution.py:154
  106.9 61.8 %copy-start = (f32[512]{0:T(512)S(1)}, f32[512]{0:T(512)}, u32[]{:S(2)}) copy-start(f32[512]{0:T(512)} %param.16) | copy-start | bytes 6148
Sparse Core Ops, SparseCore 0:
  22.7 52.2 all-gather.1
where the time goes:
time: 179 us; the launch traced here: 178 us
  waiting for transfers between devices  51.9 us (29%)
  local copies, waits for them, and re-layouts  49.3 us (28%)
  matrix products  29.8 us (17%)
  other arithmetic  20.9 us (12%)
  between operations  13.6 us (8%)
  starting transfers between devices  6.8 us (4%)
  loops' own time  6.06 us (3%)
    all_gather x1, waiting for transfers between devices, shards(): lax.all_gather(bundle, 'seq', axis=0, tiled=True)  48.4 us
    slice x1, local copies, waits for them, and re-layouts, fold_packet(): packet[:, 1, :BLK, :].reshape(step_count, key_count, heads_kv, HD)  21.4 us
    dot_general x6, matrix products, update(): jnp.einsum('kgrn,nkd->kgrd', scaled, value_tile, preferred_element_type=j...  19.7 us
    dot_general x6, matrix products, update(): jnp.einsum('kgrd,nkd->kgrn', query_tile, key_tile, preferred_element_type...  10.1 us
    unnamed x9, local copies, waits for them, and re-layouts  7.61 us
    reduce_sum x6, other arithmetic, update(): run_sum = run_sum * factor + jnp.sum(weights, axis=-1)  6.84 us
    reduce_or x8, other arithmetic, block_update(): return lax.cond(jnp.any(allowed), update, keep_state, totals)  6.15 us
    another operation x1, loops' own time, fold_packet(): lax.scan(one_step, totals, (key_part, value_part, key_scale, value_scale,...  5.54 us
  transfers between devices with their start and end apart: 3, of which 3 were waited for; matrix products, arithmetic and copies ran while one was open for 4% of the time, Pallas kernels for 0%

commit v1 on v0

v1 whole, which is shorter than its diff:
```python
import functools
import math

import jax
import jax.numpy as jnp
from jax import lax
from jax.experimental import pallas as pl
from jax.experimental.pallas import tpu as pltpu
from jax.sharding import PartitionSpec as P

QH = 64
KVH = 8
HD = 128
BLK = 64
G = QH // KVH
NEG = -1e30
MESH = pl.DeviceIdType.MESH
SCALE = math.log2(math.e) / math.sqrt(HD)


def kernel(
    dims,
    doc_ref,
    q_hbm,
    k_hbm,
    v_hbm,
    ks_ref,
    vs_ref,
    mean_ref,
    out_hbm,
    buf,
    q_vm,
    qt,
    acc,
    m_ref,
    l_ref,
    out_vm,
    bias,
    lo_ref,
    local_sem,
    out_sem,
    head_send,
    head_recv,
    send,
    recv,
):
    planes, nh, rows, hk, toks, reach = dims
    cols = hk * HD
    s = lax.axis_index("seq")
    h = lax.axis_index("head")
    z, x, c = s // 4, (s // 2) % 2, s % 2
    g = s // 2
    zdst, xdst, cdst = s + 4, s + 2 - 4 * x, s + 1 - 2 * c

    barrier = pltpu.get_barrier_semaphore()

    def greet(seq, head):
        pl.semaphore_signal(barrier, inc=1, device_id=(seq, head), device_id_type=MESH)

    for step in range(1, nh):
        greet(s, (h + step) % nh)
    greet(xdst, h)
    greet(cdst, h)

    @pl.when(z > 0)
    def _():
        greet(s - 4, h)

    @pl.when(z < planes - 1)
    def _():
        greet(s + 4, h)

    q_copy = pltpu.make_async_copy(q_hbm, q_vm, local_sem.at[0])
    q_copy.start()
    own_cols = pl.ds(pl.multiple_of(h * cols, HD), cols)
    locals_ = []
    for piece, hbm in enumerate((k_hbm, v_hbm)):
        dst = buf.at[s, pl.ds(pl.multiple_of(piece * rows + h * toks, 16), toks)]
        locals_.append(pltpu.make_async_copy(hbm.at[:, own_cols], dst, local_sem.at[1 + piece]))
        locals_[-1].start()

    pl.semaphore_wait(
        barrier,
        nh + 1 + jnp.where(z > 0, 1, 0) + jnp.where(z < planes - 1, 1, 0),
    )

    head_copies = []
    for piece, hbm in enumerate((k_hbm, v_hbm)):
        for step in range(1, nh):
            peer = (h + step) % nh
            peer_cols = pl.ds(pl.multiple_of(peer * cols, HD), cols)
            dst = buf.at[s, pl.ds(pl.multiple_of(piece * rows + h * toks, 16), toks)]
            head_copies.append(
                pltpu.make_async_remote_copy(
                    src_ref=hbm.at[:, peer_cols],
                    dst_ref=dst,
                    send_sem=head_send.at[piece, step - 1],
                    recv_sem=head_recv.at[piece, step - 1],
                    device_id=(s, peer),
                    device_id_type=MESH,
                )
            )
            head_copies[-1].start()

    per = rows // BLK
    pieces = []
    for ref in (ks_ref, vs_ref):
        sc = ref[...].astype(jnp.float32)
        pieces.append(
            jnp.concatenate(
                [jnp.broadcast_to(sc[:, i : i + 1], (per, HD)) for i in range(hk)], axis=1
            )
        )
    pieces.append(jnp.zeros((16 - 2 * per, cols), jnp.float32))
    buf[s, 2 * rows :, :] = jnp.concatenate(pieces, axis=0).astype(jnp.bfloat16)

    def part(slot, p):
        if p == 0:
            return buf.at[slot, pl.ds(0, rows)]
        return buf.at[slot, pl.ds(rows, rows + 16)]

    def copy(kind, slot, p, dst):
        return pltpu.make_async_remote_copy(
            src_ref=part(slot, p),
            dst_ref=part(slot, p),
            send_sem=send.at[kind, slot, p],
            recv_sem=recv.at[slot, p],
            device_id=(dst, h),
            device_id_type=MESH,
        )

    def need(g0, at):
        return (g0 >= 0) & (g0 <= at) & (g0 >= at - reach)

    def routes(g0, chain):
        out = [(2, need(g0, g), cdst)]
        if chain:
            up = (z + 1 < planes) & (g0 >= 0) & (g0 >= 2 * (z + 1) - reach)
            across = need(g0, 2 * z + 1 - x)
            out = [(0, up, zdst), (1, across, xdst)] + out
        return out

    def forward(g0, chain, p):
        for kind, cond, dst in routes(g0, chain):

            @pl.when(cond)
            def _(kind=kind, dst=dst):
                copy(kind, g0 * 2 + c, p, dst).start()

    def drain(g0, chain):
        for kind, cond, dst in routes(g0, chain):

            @pl.when(cond)
            def _(kind=kind, dst=dst):
                for p in range(2):
                    copy(kind, g0 * 2 + c, p, dst).wait_send()

    def arrive(slot, p):
        copy(2, slot, p, cdst).wait_recv()

    for piece in range(2):
        locals_[piece].wait()
        for step in range(1, nh):
            head_copies[piece * (nh - 1) + step - 1].wait_recv()
        forward(g, True, piece)

    pos = s * rows + lax.broadcasted_iota(jnp.int32, (1, rows), 1)
    start = jnp.int32(0)
    low = jnp.zeros((1, rows), jnp.int32)
    for j in range(doc_ref.shape[0]):
        low = jnp.where(pos >= start, start, low)
        start = start + doc_ref[j]
    lo_ref[...] = low
    m_ref[...] = jnp.full(m_ref.shape, NEG, jnp.float32)
    l_ref[...] = jnp.zeros(l_ref.shape, jnp.float32)
    acc[...] = jnp.zeros(acc.shape, jnp.float32)
    q_copy.wait()
    for i in range(hk):
        for j in range(G):
            tile = q_vm[:, (i * G + j) * HD : (i * G + j + 1) * HD]
            qt[i, :, j * rows : (j + 1) * rows] = tile.T

    keys = 2 * rows
    blocks = keys // BLK
    wide = 2 * rows

    def compute(g0):
        key_pos = g0 * keys + lax.broadcasted_iota(jnp.int32, (keys, rows), 0)
        query_pos = s * rows + lax.broadcasted_iota(jnp.int32, (keys, rows), 1)
        ok = (key_pos >= lo_ref[...]) & (key_pos <= query_pos)
        bias[...] = jnp.where(ok, 0.0, NEG)

        def one_head(i, carry):
            lanes = pl.ds(pl.multiple_of(i * HD, HD), HD)
            k = buf[pl.ds(2 * g0, 2), 0:rows, lanes].reshape(keys, HD)
            v = buf[pl.ds(2 * g0, 2), rows : 2 * rows, lanes].reshape(keys, HD)
            vt = v.T
            sc = buf[pl.ds(2 * g0, 2), 2 * rows : 2 * rows + 16, lanes].astype(jnp.float32)
            ks = sc[:, 0:per].reshape(blocks, 1, HD) * SCALE
            vs = sc[:, per : 2 * per].reshape(blocks, 1, HD)
            ks = jnp.concatenate([ks, ks], axis=2)
            vs = jnp.concatenate([vs, vs], axis=2)
            mask = bias[...]
            mask = jnp.concatenate([mask, mask], axis=1)
            for j in range(G * rows // wide):
                at = slice(j * wide, (j + 1) * wide)
                sco = jnp.dot(k, qt[i, :, at], preferred_element_type=jnp.float32)
                sco = (sco.reshape(blocks, BLK, wide) * ks).reshape(keys, wide) + mask
                old = m_ref[i, :, at]
                new = jnp.maximum(old, jnp.max(sco, axis=0, keepdims=True))
                w = jnp.exp2(sco - new)
                fac = jnp.exp2(old - new)
                m_ref[i, :, at] = new
                l_ref[i, :, at] = l_ref[i, :, at] * fac + jnp.sum(w, axis=0, keepdims=True)
                wb = (w.reshape(blocks, BLK, wide) * vs).reshape(keys, wide).astype(jnp.bfloat16)
                acc[i, :, at] = acc[i, :, at] * fac + jnp.dot(
                    vt, wb, preferred_element_type=jnp.float32
                )
            return carry

        lax.fori_loop(0, hk, one_head, 0)

    def sibling(g0):
        for p in range(2):
            arrive(g0 * 2 + 1 - c, p)

    def across_block(dz):
        g0 = 2 * (z - dz) + 1 - x

        @pl.when(need(g0, g))
        def _():
            for p in range(2):
                arrive(g0 * 2 + c, p)
                forward(g0, False, p)
            sibling(g0)
            compute(g0)

    sibling(g)
    compute(g)
    last = (reach + 1) // 2

    def one_plane(dz, carry):
        g0 = 2 * (z - dz) + x

        @pl.when((g0 >= 0) & (g0 >= 2 * z - reach))
        def _():
            for p in range(2):
                arrive(g0 * 2 + c, p)
                forward(g0, True, p)

        across_block(dz - 1)

        @pl.when(need(g0, g))
        def _():
            sibling(g0)
            compute(g0)

        return carry

    lax.fori_loop(1, last + 1, one_plane, 0)
    across_block(last)

    outs = []
    for i in range(hk):
        for j in range(G):
            at = slice(j * rows, (j + 1) * rows)
            o = acc[i, :, at] * (1.0 / l_ref[i, :, at])
            o = o.T + mean_ref[:, i * HD : (i + 1) * HD]
            out_vm[:, (i * G + j) * HD : (i * G + j + 1) * HD] = o.astype(jnp.bfloat16)
        span = pl.ds(i * G * HD, G * HD)
        outs.append(pltpu.make_async_copy(out_vm.at[:, span], out_hbm.at[:, span], out_sem.at[i]))
        outs[-1].start()

    for one in head_copies:
        one.wait_send()

    def settle(dz, carry):
        g0 = 2 * (z - dz) + x

        @pl.when((dz == 0) | (g0 >= 0) & (g0 >= 2 * z - reach))
        def _():
            drain(g0, True)

        g1 = 2 * (z - dz) + 1 - x

        @pl.when(need(g1, g))
        def _():
            drain(g1, False)

        return carry

    lax.fori_loop(0, last + 1, settle, 0)
    for one in outs:
        one.wait()


def shards(queries, key_tokens, value_tokens, key_scales, value_scales, value_means, doc_lengths, nseq, nh):
    rows, width = queries.shape
    toks = key_tokens.shape[0]
    hk = width // (G * HD)
    cols = hk * HD
    most = nseq * rows * 5 // 8
    window = (most - 1 + rows - 1) // rows
    reach = (window + 1) // 2
    dims = (nseq // 4, nh, rows, hk, toks, reach)
    anyspace = pl.BlockSpec(memory_space=pl.ANY)
    vmem = pl.BlockSpec(memory_space=pltpu.VMEM)
    smem = pl.BlockSpec(memory_space=pltpu.SMEM)
    dma = pltpu.SemaphoreType.DMA
    return pl.pallas_call(
        functools.partial(kernel, dims),
        out_shape=jax.ShapeDtypeStruct((rows, width), jnp.bfloat16),
        in_specs=[smem, anyspace, anyspace, anyspace, vmem, vmem, vmem],
        out_specs=anyspace,
        scratch_shapes=[
            pltpu.VMEM((nseq, 2 * rows + 16, cols), jnp.bfloat16),
            pltpu.VMEM((rows, width), jnp.bfloat16),
            pltpu.VMEM((hk, HD, G * rows), jnp.bfloat16),
            pltpu.VMEM((hk, HD, G * rows), jnp.float32),
            pltpu.VMEM((hk, 1, G * rows), jnp.float32),
            pltpu.VMEM((hk, 1, G * rows), jnp.float32),
            pltpu.VMEM((rows, width), jnp.bfloat16),
            pltpu.VMEM((2 * rows, rows), jnp.float32),
            pltpu.VMEM((1, rows), jnp.int32),
            dma((3,)),
            dma((hk,)),
            dma((2, max(nh - 1, 1))),
            dma((2, max(nh - 1, 1))),
            dma((3, nseq, 2)),
            dma((nseq, 2)),
        ],
        compiler_params=pltpu.CompilerParams(
            collective_id=0, has_side_effects=True, vmem_limit_bytes=48 * 1024 * 1024
        ),
        cost_estimate=pl.CostEstimate(
            flops=4 * rows * width * 2 * rows * (reach + 1),
            bytes_accessed=4 * rows * width,
            transcendentals=0,
        ),
        name="attend",
    )(
        doc_lengths,
        queries,
        key_tokens,
        value_tokens,
        key_scales,
        value_scales,
        value_means.reshape(1, cols),
    )


def solution(mesh):
    in_specs = (
        P("seq", "head"),
        P(("seq", "head"), None),
        P(("seq", "head"), None),
        P("seq", "head"),
        P("seq", "head"),
        P("head"),
        P(),
    )
    body = functools.partial(shards, nseq=mesh.shape["seq"], nh=mesh.shape["head"])
    return jax.shard_map(body, mesh=mesh, in_specs=in_specs, out_specs=P("seq", "head"), check_vma=False)
```

time: 179 us -> 58.7 us (0.33)
  Pallas kernels: 0 us -> 53.1 us
  waiting for transfers between devices: 51.9 us -> 0 us
  local copies, waits for them, and re-layouts: 49.3 us -> 5.37 us
  matrix products: 29.8 us -> 0 us
  other arithmetic: 20.9 us -> 0 us
  between operations: 13.6 us -> 0.02 us
  starting transfers between devices: 6.8 us -> 0 us
  loops' own time: 6.06 us -> 0 us
    pallas_call x0 -> x1, Pallas kernels: none -> 53.1 us  [shards(): pl.pallas_call(functools.partial(kernel, dims), out_shape=jax.ShapeDtypeS...]
    all_gather x1 -> x0, waiting for transfers between devices: 48.4 us -> none  [shards(): lax.all_gather(bundle, 'seq', axis=0, tiled=True)]
    dot_general x12 -> x0, matrix products: 29.8 us -> none  [the longest x6 19.7 us: update(): jnp.einsum('kgrn,nkd->kgrd', scaled, value_tile, preferred_element_type=j...]
    slice x2 -> x0, local copies, waits for them, and re-layouts: 22.6 us -> none  [the longest x1 21.4 us: fold_packet(): packet[:, 1, :BLK, :].reshape(step_count, key_count, heads_kv, HD)]
    another operation x20 -> x0, local copies, waits for them, and re-layouts: 7.97 us -> none  [the longest x1 2.55 us: fold_packet(): packet[:, 0, :BLK, :].reshape(step_count, key_count, heads_kv, HD)]
    reduce_sum x15 -> x0, other arithmetic: 7.68 us -> none  [the longest x6 6.84 us: update(): run_sum = run_sum * factor + jnp.sum(weights, axis=-1)]
    all_to_all x2 -> x0, starting transfers between devices: 6.76 us -> none  [the longest x1 3.38 us: shards(): lax.all_to_all(value_tokens, 'head', split_axis=1, concat_axis=0, tiled=T...]
    reduce_or x8 -> x0, other arithmetic: 6.15 us -> none  [block_update(): return lax.cond(jnp.any(allowed), update, keep_state, totals)]
  transfers between devices with their start and end apart: 3 -> 0, of which waited for: 3 -> 0; matrix products, arithmetic and copies ran while one was open for 4% -> 0% of each run, Pallas kernels for 0% -> 0%
where the time goes in v1:
time: 58.7 us; the launch traced here: 58.5 us
  Pallas kernels  53.1 us (90%)
  local copies, waits for them, and re-layouts  5.37 us (9%)
    pallas_call x1, Pallas kernels, shards(): pl.pallas_call(functools.partial(kernel, dims), out_shape=jax.ShapeDtypeS...  53.1 us
    unnamed x15, local copies, waits for them, and re-layouts  5.37 us

profile of v1, /device:TPU:25, one launch (start us, length us, event | category | flops | bytes accessed | tf_op | source)
XLA Modules:
  0.0 58.5 jit_solution(5738446260672983933)
XLA Ops:
  0.0 0.0 copy-start.4
  0.0 0.0 copy-start.6
  0.0 0.0 copy-start.5
  0.0 0.6 %copy-done.4 = s32[64]{0:T(128)S(1)} copy-done((s32[64]{0:T(128)S(1)}, s32[64]{0:T(128)}, u32[]{:S(2)}) %copy-start.4) | copy-done | bytes 280
  0.7 0.0 copy-done.6
  0.7 0.0 copy-done.5
  0.7 0.0 copy-start
  0.7 1.2 %copy-done = bf16[128,4096]{1,0:T(8,128)(2,1)S(1)} copy-done((bf16[128,4096]{1,0:T(8,128)(2,1)S(1)}, bf16[128,4096]{1,0:T(8,128)(2,1)}, u32[]{:S(2)}) %copy-start) | copy-done | bytes 1048600
  1.9 0.0 copy-start.1
  1.9 0.9 %copy-done.1 = bf16[64,1024]{1,0:T(8,128)(2,1)S(1)} copy-done((bf16[64,1024]{1,0:T(8,128)(2,1)S(1)}, bf16[64,1024]{1,0:T(8,128)(2,1)}, u32[]{:S(2)}) %copy-start.1) | copy-done | bytes 131096
  2.8 0.0 copy-start.2
  2.8 0.9 %copy-done.2 = bf16[64,1024]{1,0:T(8,128)(2,1)S(1)} copy-done((bf16[64,1024]{1,0:T(8,128)(2,1)S(1)}, bf16[64,1024]{1,0:T(8,128)(2,1)}, u32[]{:S(2)}) %copy-start.2) | copy-done | bytes 131096
  3.7 0.0 copy-start.3
  3.7 0.7 %copy-done.3 = f32[512]{0:T(512)S(1)} copy-done((f32[512]{0:T(512)S(1)}, f32[512]{0:T(512)}, u32[]{:S(2)}) %copy-start.3) | copy-done | bytes 2072
  4.4 53.1 %attend.1 = bf16[128,4096]{1,0:T(8,128)(2,1)S(1)} custom-call(s32[64]{0:T(128)S(1)} %copy-done.4, bf16[128,4096]{1,0:T(8,128)(2,1)S(1)} %copy-done, bf16[64,1024]{1,0:T(8,128)(2,1)S(1)} %copy-done.1, bf16[64,1024]{1,0:T(8,128)(2,1)S(1)} %copy-done.2, bf16[2,4]{1,0:T(2,128)(2,1)S(1)} %copy-done.5, bf16[2,4]{1,0:T(2,128)(2,1)S(1)} %copy-done.6, ...), custom_call_target="tpu_custom_call" | custom-call | flops 3221225472 | bytes 2097152 | tf_op jit(solution)/shard_map/attend/pallas_call | solution.py:310
  57.5 1.0 %copy.9 = bf16[128,4096]{1,0:T(8,128)(2,1)} copy(bf16[128,4096]{1,0:T(8,128)(2,1)S(1)} %attend.1) | data formatting | bytes 2097152
Async XLA Ops:
  0.0 0.7 %copy-start.4 = (s32[64]{0:T(128)S(1)}, s32[64]{0:T(128)}, u32[]{:S(2)}) copy-start(s32[64]{0:T(128)} %doc_ref.1) | copy-start | bytes 772
  0.0 0.7 %copy-start.6 = (bf16[2,4]{1,0:T(2,128)(2,1)S(1)}, bf16[2,4]{1,0:T(2,128)(2,1)}, u32[]{:S(2)}) copy-start(bf16[2,4]{1,0:T(2,128)(2,1)} %vs_ref.1) | copy-start | bytes 52
  0.0 0.7 %copy-start.5 = (bf16[2,4]{1,0:T(2,128)(2,1)S(1)}, bf16[2,4]{1,0:T(2,128)(2,1)}, u32[]{:S(2)}) copy-start(bf16[2,4]{1,0:T(2,128)(2,1)} %ks_ref.1) | copy-start | bytes 52
  0.7 1.2 %copy-start = (bf16[128,4096]{1,0:T(8,128)(2,1)S(1)}, bf16[128,4096]{1,0:T(8,128)(2,1)}, u32[]{:S(2)}) copy-start(bf16[128,4096]{1,0:T(8,128)(2,1)} %q_hbm.1) | copy-start | bytes 3145732
  1.9 0.9 %copy-start.1 = (bf16[64,1024]{1,0:T(8,128)(2,1)S(1)}, bf16[64,1024]{1,0:T(8,128)(2,1)}, u32[]{:S(2)}) copy-start(bf16[64,1024]{1,0:T(8,128)(2,1)} %k_hbm.1) | copy-start | bytes 393220
  2.8 0.9 %copy-start.2 = (bf16[64,1024]{1,0:T(8,128)(2,1)S(1)}, bf16[64,1024]{1,0:T(8,128)(2,1)}, u32[]{:S(2)}) copy-start(bf16[64,1024]{1,0:T(8,128)(2,1)} %v_hbm.1) | copy-start | bytes 393220
  3.7 0.7 %copy-start.3 = (f32[512]{0:T(512)S(1)}, f32[512]{0:T(512)}, u32[]{:S(2)}) copy-start(f32[512]{0:T(512)} %param.12) | copy-start | bytes 6148

commit v2 on v1

--- a/solution.py
+++ b/solution.py
@@ -20,25 +20,27 @@
 
 def kernel(
     dims,
-    doc_ref,
+    doc_hbm,
     q_hbm,
     k_hbm,
     v_hbm,
+    ks_hbm,
+    vs_hbm,
+    mean_hbm,
+    out_ref,
+    buf,
+    q_vm,
+    doc_ref,
     ks_ref,
     vs_ref,
     mean_ref,
-    out_hbm,
-    buf,
-    q_vm,
     qt,
     acc,
     m_ref,
-    l_ref,
-    out_vm,
+    mean_t,
     bias,
     lo_ref,
     local_sem,
-    out_sem,
     head_send,
     head_recv,
     send,
@@ -70,8 +72,12 @@
     def _():
         greet(s + 4, h)
 
-    q_copy = pltpu.make_async_copy(q_hbm, q_vm, local_sem.at[0])
-    q_copy.start()
+    small = []
+    for n, (src, dst) in enumerate(
+        ((ks_hbm, ks_ref), (vs_hbm, vs_ref), (doc_hbm, doc_ref), (mean_hbm, mean_ref))
+    ):
+        small.append(pltpu.make_async_copy(src, dst, local_sem.at[3 + n]))
+        small[-1].start()
     own_cols = pl.ds(pl.multiple_of(h * cols, HD), cols)
     locals_ = []
     for piece, hbm in enumerate((k_hbm, v_hbm)):
@@ -79,6 +85,8 @@
         locals_.append(pltpu.make_async_copy(hbm.at[:, own_cols], dst, local_sem.at[1 + piece]))
         locals_[-1].start()
 
+    q_copy = pltpu.make_async_copy(q_hbm, q_vm, local_sem.at[0])
+    q_copy.start()
     pl.semaphore_wait(
         barrier,
         nh + 1 + jnp.where(z > 0, 1, 0) + jnp.where(z < planes - 1, 1, 0),
@@ -104,6 +112,8 @@
 
     per = rows // BLK
     pieces = []
+    small[0].wait()
+    small[1].wait()
     for ref in (ks_ref, vs_ref):
         sc = ref[...].astype(jnp.float32)
         pieces.append(
@@ -164,6 +174,8 @@
             head_copies[piece * (nh - 1) + step - 1].wait_recv()
         forward(g, True, piece)
 
+    small[2].wait()
+    small[3].wait()
     pos = s * rows + lax.broadcasted_iota(jnp.int32, (1, rows), 1)
     start = jnp.int32(0)
     low = jnp.zeros((1, rows), jnp.int32)
@@ -172,13 +184,13 @@
         start = start + doc_ref[j]
     lo_ref[...] = low
     m_ref[...] = jnp.full(m_ref.shape, NEG, jnp.float32)
-    l_ref[...] = jnp.zeros(l_ref.shape, jnp.float32)
     acc[...] = jnp.zeros(acc.shape, jnp.float32)
     q_copy.wait()
     for i in range(hk):
         for j in range(G):
             tile = q_vm[:, (i * G + j) * HD : (i * G + j + 1) * HD]
             qt[i, :, j * rows : (j + 1) * rows] = tile.T
+        mean_t[i] = jnp.broadcast_to(mean_ref[:, i * HD : (i + 1) * HD], (rows, HD)).T
 
     keys = 2 * rows
     blocks = keys // BLK
@@ -190,35 +202,56 @@
         ok = (key_pos >= lo_ref[...]) & (key_pos <= query_pos)
         bias[...] = jnp.where(ok, 0.0, NEG)
 
-        def one_head(i, carry):
-            lanes = pl.ds(pl.multiple_of(i * HD, HD), HD)
+        mask = jnp.concatenate([bias[...], bias[...]], axis=1)
+        units = [(i, j) for i in range(hk) for j in range(G * rows // wide)]
+        lane = lax.broadcasted_iota(jnp.int32, (1, HD), 1)
+        sub = lax.broadcasted_iota(jnp.int32, (16, keys), 0)
+
+        def head_of(i):
+            lanes = slice(i * HD, (i + 1) * HD)
             k = buf[pl.ds(2 * g0, 2), 0:rows, lanes].reshape(keys, HD)
             v = buf[pl.ds(2 * g0, 2), rows : 2 * rows, lanes].reshape(keys, HD)
-            vt = v.T
             sc = buf[pl.ds(2 * g0, 2), 2 * rows : 2 * rows + 16, lanes].astype(jnp.float32)
             ks = sc[:, 0:per].reshape(blocks, 1, HD) * SCALE
             vs = sc[:, per : 2 * per].reshape(blocks, 1, HD)
+            inv = 1.0 / vs
+            inv = jnp.concatenate(
+                [jnp.where(lane < BLK, inv[2 * n], inv[2 * n + 1]) for n in range(2)], axis=1
+            )
+            high = inv.astype(jnp.bfloat16).astype(jnp.float32)
+            both = jnp.where(sub == 0, high, jnp.where(sub == 1, inv - high, 0.0))
+            vt = jnp.concatenate([v.T, both.astype(jnp.bfloat16)], axis=0)
+            lvs = jnp.log2(vs)
             ks = jnp.concatenate([ks, ks], axis=2)
-            vs = jnp.concatenate([vs, vs], axis=2)
-            mask = bias[...]
-            mask = jnp.concatenate([mask, mask], axis=1)
-            for j in range(G * rows // wide):
-                at = slice(j * wide, (j + 1) * wide)
-                sco = jnp.dot(k, qt[i, :, at], preferred_element_type=jnp.float32)
-                sco = (sco.reshape(blocks, BLK, wide) * ks).reshape(keys, wide) + mask
-                old = m_ref[i, :, at]
-                new = jnp.maximum(old, jnp.max(sco, axis=0, keepdims=True))
-                w = jnp.exp2(sco - new)
-                fac = jnp.exp2(old - new)
-                m_ref[i, :, at] = new
-                l_ref[i, :, at] = l_ref[i, :, at] * fac + jnp.sum(w, axis=0, keepdims=True)
-                wb = (w.reshape(blocks, BLK, wide) * vs).reshape(keys, wide).astype(jnp.bfloat16)
-                acc[i, :, at] = acc[i, :, at] * fac + jnp.dot(
-                    vt, wb, preferred_element_type=jnp.float32
-                )
-            return carry
-
-        lax.fori_loop(0, hk, one_head, 0)
+            lvs = jnp.concatenate([lvs, lvs], axis=2)
+            return k, vt, ks, lvs
+
+        def score(unit, head):
+            i, j = unit
+            return jnp.dot(
+                head[0], qt[i, :, j * wide : (j + 1) * wide], preferred_element_type=jnp.float32
+            )
+
+        heads = {0: head_of(0)}
+        ahead = score(units[0], heads[0])
+        for n, (i, j) in enumerate(units):
+            raw = ahead
+            if n + 1 < len(units):
+                after = units[n + 1][0]
+                if after not in heads:
+                    heads[after] = head_of(after)
+                ahead = score(units[n + 1], heads[after])
+            _, vt, ks, lvs = heads[i]
+            at = slice(j * wide, (j + 1) * wide)
+            sco = (raw.reshape(blocks, BLK, wide) * ks).reshape(keys, wide) + mask
+            old = m_ref[i, :, at]
+            new = jnp.maximum(old, jnp.max(sco, axis=0, keepdims=True))
+            fac = jnp.exp2(old - new)
+            m_ref[i, :, at] = new
+            w = jnp.exp2(sco.reshape(blocks, BLK, wide) - (new.reshape(1, 1, wide) - lvs))
+            wb = w.reshape(keys, wide).astype(jnp.bfloat16)
+            got = jnp.dot(vt, wb, preferred_element_type=jnp.float32)
+            acc[i, :, at] = acc[i, :, at] * fac + got[: HD + 8]
 
     def sibling(g0):
         for p in range(2):
@@ -260,16 +293,12 @@
     lax.fori_loop(1, last + 1, one_plane, 0)
     across_block(last)
 
-    outs = []
     for i in range(hk):
         for j in range(G):
             at = slice(j * rows, (j + 1) * rows)
-            o = acc[i, :, at] * (1.0 / l_ref[i, :, at])
-            o = o.T + mean_ref[:, i * HD : (i + 1) * HD]
-            out_vm[:, (i * G + j) * HD : (i * G + j + 1) * HD] = o.astype(jnp.bfloat16)
-        span = pl.ds(i * G * HD, G * HD)
-        outs.append(pltpu.make_async_copy(out_vm.at[:, span], out_hbm.at[:, span], out_sem.at[i]))
-        outs[-1].start()
+            total = acc[i, HD : HD + 1, at] + acc[i, HD + 1 : HD + 2, at]
+            o = acc[i, :HD, at] * (1.0 / total) + mean_t[i]
+            out_ref[:, (i * G + j) * HD : (i * G + j + 1) * HD] = o.astype(jnp.bfloat16).T
 
     for one in head_copies:
         one.wait_send()
@@ -290,8 +319,6 @@
         return carry
 
     lax.fori_loop(0, last + 1, settle, 0)
-    for one in outs:
-        one.wait()
 
 
 def shards(queries, key_tokens, value_tokens, key_scales, value_scales, value_means, doc_lengths, nseq, nh):
@@ -303,34 +330,35 @@
     window = (most - 1 + rows - 1) // rows
     reach = (window + 1) // 2
     dims = (nseq // 4, nh, rows, hk, toks, reach)
-    anyspace = pl.BlockSpec(memory_space=pl.ANY)
+    hbm = pl.BlockSpec(memory_space=pltpu.HBM)
     vmem = pl.BlockSpec(memory_space=pltpu.VMEM)
-    smem = pl.BlockSpec(memory_space=pltpu.SMEM)
     dma = pltpu.SemaphoreType.DMA
     return pl.pallas_call(
         functools.partial(kernel, dims),
         out_shape=jax.ShapeDtypeStruct((rows, width), jnp.bfloat16),
-        in_specs=[smem, anyspace, anyspace, anyspace, vmem, vmem, vmem],
-        out_specs=anyspace,
+        in_specs=[hbm] * 7,
+        out_specs=vmem,
         scratch_shapes=[
             pltpu.VMEM((nseq, 2 * rows + 16, cols), jnp.bfloat16),
             pltpu.VMEM((rows, width), jnp.bfloat16),
+            pltpu.SMEM(doc_lengths.shape, jnp.int32),
+            pltpu.VMEM(key_scales.shape, jnp.bfloat16),
+            pltpu.VMEM(value_scales.shape, jnp.bfloat16),
+            pltpu.VMEM((1, cols), jnp.float32),
             pltpu.VMEM((hk, HD, G * rows), jnp.bfloat16),
-            pltpu.VMEM((hk, HD, G * rows), jnp.float32),
+            pltpu.VMEM((hk, HD + 8, G * rows), jnp.float32),
             pltpu.VMEM((hk, 1, G * rows), jnp.float32),
-            pltpu.VMEM((hk, 1, G * rows), jnp.float32),
-            pltpu.VMEM((rows, width), jnp.bfloat16),
+            pltpu.VMEM((hk, HD, rows), jnp.float32),
             pltpu.VMEM((2 * rows, rows), jnp.float32),
             pltpu.VMEM((1, rows), jnp.int32),
-            dma((3,)),
-            dma((hk,)),
+            dma((7,)),
             dma((2, max(nh - 1, 1))),
             dma((2, max(nh - 1, 1))),
             dma((3, nseq, 2)),
             dma((nseq, 2)),
         ],
         compiler_params=pltpu.CompilerParams(
-            collective_id=0, has_side_effects=True, vmem_limit_bytes=48 * 1024 * 1024
+            collective_id=0, has_side_effects=True, vmem_limit_bytes=62 * 1024 * 1024
         ),
         cost_estimate=pl.CostEstimate(
             flops=4 * rows * width * 2 * rows * (reach + 1),

time: 58.7 us -> 41.1 us (0.70)
  Pallas kernels: 53.1 us -> 38.6 us
  local copies, waits for them, and re-layouts: 5.37 us -> 2.29 us
    pallas_call x1, Pallas kernels: 53.1 us -> 38.6 us  [shards(): pl.pallas_call(functools.partial(kernel, dims), out_shape=jax.ShapeDtypeS...]
    unnamed x15 -> x1, local copies, waits for them, and re-layouts: 5.37 us -> 2.29 us
where the time goes in v2:
time: 41.1 us; the launch traced here: 40.9 us
  Pallas kernels  38.6 us (94%)
  local copies, waits for them, and re-layouts  2.29 us (6%)
    pallas_call x1, Pallas kernels, shards(): pl.pallas_call(functools.partial(kernel, dims), out_shape=jax.ShapeDtypeS...  38.6 us
    unnamed x1, local copies, waits for them, and re-layouts  2.29 us

profile of v2, /device:TPU:25, one launch (start us, length us, event | category | flops | bytes accessed | tf_op | source)
XLA Modules:
  0.0 40.9 jit_solution(17270346452306347326)
XLA Ops:
  0.0 38.6 %attend.1 = bf16[128,4096]{1,0:T(8,128)(2,1)} custom-call(s32[64]{0:T(128)} %doc_hbm.1, bf16[128,4096]{1,0:T(8,128)(2,1)} %q_hbm.1, bf16[64,1024]{1,0:T(8,128)(2,1)} %k_hbm.1, bf16[64,1024]{1,0:T(8,128)(2,1)} %v_hbm.1, bf16[2,4]{1,0:T(2,128)(2,1)} %ks_hbm.1, bf16[2,4]{1,0:T(2,128)(2,1)} %vs_hbm.1, f32[1,512]{1,0:T(1,128)} %bitcast.1), custom_call_target="tpu_custom_call" | custom-call | flops 3221225472 | bytes 2097152 | tf_op jit(solution)/shard_map/attend/pallas_call | solution.py:336
  38.6 2.3 %copy.9 = bf16[128,4096]{1,0:T(8,128)(2,1)} copy(bf16[128,4096]{1,0:T(8,128)(2,1)} %attend.1) | data formatting | bytes 2097152

commit v3 on v2

--- a/solution.py
+++ b/solution.py
@@ -41,6 +41,7 @@
     bias,
     lo_ref,
     local_sem,
+    own_sem,
     head_send,
     head_recv,
     send,
@@ -78,12 +79,19 @@
     ):
         small.append(pltpu.make_async_copy(src, dst, local_sem.at[3 + n]))
         small[-1].start()
-    own_cols = pl.ds(pl.multiple_of(h * cols, HD), cols)
-    locals_ = []
-    for piece, hbm in enumerate((k_hbm, v_hbm)):
-        dst = buf.at[s, pl.ds(pl.multiple_of(piece * rows + h * toks, 16), toks)]
-        locals_.append(pltpu.make_async_copy(hbm.at[:, own_cols], dst, local_sem.at[1 + piece]))
-        locals_[-1].start()
+    def own_part(piece, i):
+        return buf.at[s, i, pl.ds(pl.multiple_of(piece * rows + h * toks, 16), toks)]
+
+    def columns(owner, i):
+        return pl.ds(pl.multiple_of(owner * cols + i * HD, HD), HD)
+
+    locals_ = {}
+    for i in range(hk):
+        for piece, hbm in enumerate((k_hbm, v_hbm)):
+            locals_[piece, i] = pltpu.make_async_copy(
+                hbm.at[:, columns(h, i)], own_part(piece, i), own_sem.at[piece, i]
+            )
+            locals_[piece, i].start()
 
     q_copy = pltpu.make_async_copy(q_hbm, q_vm, local_sem.at[0])
     q_copy.start()
@@ -92,42 +100,33 @@
         nh + 1 + jnp.where(z > 0, 1, 0) + jnp.where(z < planes - 1, 1, 0),
     )
 
-    head_copies = []
-    for piece, hbm in enumerate((k_hbm, v_hbm)):
-        for step in range(1, nh):
-            peer = (h + step) % nh
-            peer_cols = pl.ds(pl.multiple_of(peer * cols, HD), cols)
-            dst = buf.at[s, pl.ds(pl.multiple_of(piece * rows + h * toks, 16), toks)]
-            head_copies.append(
-                pltpu.make_async_remote_copy(
-                    src_ref=hbm.at[:, peer_cols],
-                    dst_ref=dst,
-                    send_sem=head_send.at[piece, step - 1],
-                    recv_sem=head_recv.at[piece, step - 1],
+    head_copies = {}
+    for i in range(hk):
+        for piece, hbm in enumerate((k_hbm, v_hbm)):
+            for step in range(1, nh):
+                peer = (h + step) % nh
+                one = pltpu.make_async_remote_copy(
+                    src_ref=hbm.at[:, columns(peer, i)],
+                    dst_ref=own_part(piece, i),
+                    send_sem=head_send.at[piece, i, step - 1],
+                    recv_sem=head_recv.at[piece, i, step - 1],
                     device_id=(s, peer),
                     device_id_type=MESH,
                 )
-            )
-            head_copies[-1].start()
+                head_copies[piece, i, step] = one
+                one.start()
 
     per = rows // BLK
-    pieces = []
     small[0].wait()
     small[1].wait()
-    for ref in (ks_ref, vs_ref):
-        sc = ref[...].astype(jnp.float32)
-        pieces.append(
-            jnp.concatenate(
-                [jnp.broadcast_to(sc[:, i : i + 1], (per, HD)) for i in range(hk)], axis=1
-            )
-        )
-    pieces.append(jnp.zeros((16 - 2 * per, cols), jnp.float32))
-    buf[s, 2 * rows :, :] = jnp.concatenate(pieces, axis=0).astype(jnp.bfloat16)
+    both_scales = [ref[...].astype(jnp.float32) for ref in (ks_ref, vs_ref)]
+    for i in range(hk):
+        scale_rows = [jnp.broadcast_to(sc[:, i : i + 1], (per, HD)) for sc in both_scales]
+        scale_rows.append(jnp.zeros((16 - 2 * per, HD), jnp.float32))
+        buf[s, i, 2 * rows :, :] = jnp.concatenate(scale_rows, axis=0).astype(jnp.bfloat16)
 
     def part(slot, p):
-        if p == 0:
-            return buf.at[slot, pl.ds(0, rows)]
-        return buf.at[slot, pl.ds(rows, rows + 16)]
+        return buf.at[slot, p]
 
     def copy(kind, slot, p, dst):
         return pltpu.make_async_remote_copy(
@@ -142,13 +141,22 @@
     def need(g0, at):
         return (g0 >= 0) & (g0 <= at) & (g0 >= at - reach)
 
+    def other_way(g0, plane):
+        return (c == 0) & (g0 == 2 * plane - reach)
+
+    def held(g0):
+        return (g0 >= 0) & (g0 >= 2 * z - reach) & ((x == 0) | jnp.logical_not(other_way(g0, z)))
+
     def routes(g0, chain):
         out = [(2, need(g0, g), cdst)]
+        top = z + 1 < planes
+        turned = other_way(g0, z + 1)
         if chain:
-            up = (z + 1 < planes) & (g0 >= 0) & (g0 >= 2 * (z + 1) - reach)
+            up = top & (g0 >= 0) & (g0 >= 2 * (z + 1) - reach)
+            up = up & ((x == 0) | jnp.logical_not(turned))
             across = need(g0, 2 * z + 1 - x)
-            out = [(0, up, zdst), (1, across, xdst)] + out
-        return out
+            return [(0, up, zdst), (1, across, xdst)] + out
+        return [(0, top & (x == 0) & turned & need(g0, g), zdst)] + out
 
     def forward(g0, chain, p):
         for kind, cond, dst in routes(g0, chain):
@@ -157,22 +165,27 @@
             def _(kind=kind, dst=dst):
                 copy(kind, g0 * 2 + c, p, dst).start()
 
-    def drain(g0, chain):
+    def drain(g0, chain, pieces, kinds=(0, 1, 2)):
         for kind, cond, dst in routes(g0, chain):
+            if kind not in kinds:
+                continue
 
             @pl.when(cond)
             def _(kind=kind, dst=dst):
-                for p in range(2):
+                for p in pieces:
                     copy(kind, g0 * 2 + c, p, dst).wait_send()
 
     def arrive(slot, p):
         copy(2, slot, p, cdst).wait_recv()
 
-    for piece in range(2):
-        locals_[piece].wait()
-        for step in range(1, nh):
-            head_copies[piece * (nh - 1) + step - 1].wait_recv()
-        forward(g, True, piece)
+    def own_piece(i):
+        for piece in range(2):
+            locals_[piece, i].wait()
+            for step in range(1, nh):
+                head_copies[piece, i, step].wait_recv()
+        forward(g, True, i)
+
+    own_piece(0)
 
     small[2].wait()
     small[3].wait()
@@ -196,22 +209,22 @@
     blocks = keys // BLK
     wide = 2 * rows
 
-    def compute(g0):
+    def set_mask(g0):
         key_pos = g0 * keys + lax.broadcasted_iota(jnp.int32, (keys, rows), 0)
         query_pos = s * rows + lax.broadcasted_iota(jnp.int32, (keys, rows), 1)
         ok = (key_pos >= lo_ref[...]) & (key_pos <= query_pos)
         bias[...] = jnp.where(ok, 0.0, NEG)
 
+    def compute(g0, i):
         mask = jnp.concatenate([bias[...], bias[...]], axis=1)
-        units = [(i, j) for i in range(hk) for j in range(G * rows // wide)]
+        units = [(i, j) for j in range(G * rows // wide)]
         lane = lax.broadcasted_iota(jnp.int32, (1, HD), 1)
         sub = lax.broadcasted_iota(jnp.int32, (16, keys), 0)
 
         def head_of(i):
-            lanes = slice(i * HD, (i + 1) * HD)
-            k = buf[pl.ds(2 * g0, 2), 0:rows, lanes].reshape(keys, HD)
-            v = buf[pl.ds(2 * g0, 2), rows : 2 * rows, lanes].reshape(keys, HD)
-            sc = buf[pl.ds(2 * g0, 2), 2 * rows : 2 * rows + 16, lanes].astype(jnp.float32)
+            k = buf[pl.ds(2 * g0, 2), i, 0:rows, :].reshape(keys, HD)
+            v = buf[pl.ds(2 * g0, 2), i, rows : 2 * rows, :].reshape(keys, HD)
+            sc = buf[pl.ds(2 * g0, 2), i, 2 * rows : 2 * rows + 16, :].astype(jnp.float32)
             ks = sc[:, 0:per].reshape(blocks, 1, HD) * SCALE
             vs = sc[:, per : 2 * per].reshape(blocks, 1, HD)
             inv = 1.0 / vs
@@ -232,16 +245,13 @@
                 head[0], qt[i, :, j * wide : (j + 1) * wide], preferred_element_type=jnp.float32
             )
 
-        heads = {0: head_of(0)}
-        ahead = score(units[0], heads[0])
+        head = head_of(i)
+        _, vt, ks, lvs = head
+        ahead = score(units[0], head)
         for n, (i, j) in enumerate(units):
             raw = ahead
             if n + 1 < len(units):
-                after = units[n + 1][0]
-                if after not in heads:
-                    heads[after] = head_of(after)
-                ahead = score(units[n + 1], heads[after])
-            _, vt, ks, lvs = heads[i]
+                ahead = score(units[n + 1], head)
             at = slice(j * wide, (j + 1) * wide)
             sco = (raw.reshape(blocks, BLK, wide) * ks).reshape(keys, wide) + mask
             old = m_ref[i, :, at]
@@ -253,45 +263,52 @@
             got = jnp.dot(vt, wb, preferred_element_type=jnp.float32)
             acc[i, :, at] = acc[i, :, at] * fac + got[: HD + 8]
 
-    def sibling(g0):
-        for p in range(2):
-            arrive(g0 * 2 + 1 - c, p)
-
-    def across_block(dz):
-        g0 = 2 * (z - dz) + 1 - x
-
+    def sibling(g0, p):
+        arrive(g0 * 2 + 1 - c, p)
+
+    def across_piece(g0, p):
         @pl.when(need(g0, g))
         def _():
-            for p in range(2):
-                arrive(g0 * 2 + c, p)
-                forward(g0, False, p)
-            sibling(g0)
-            compute(g0)
-
-    sibling(g)
-    compute(g)
+            arrive(g0 * 2 + c, p)
+            forward(g0, False, p)
+            sibling(g0, p)
+            if p == 0:
+                set_mask(g0)
+            compute(g0, p)
+
+    set_mask(g)
+    for i in range(hk):
+        if i + 1 < hk:
+            drain(g, True, (i,), (0, 1))
+            own_piece(i + 1)
+        sibling(g, i)
+        compute(g, i)
     last = (reach + 1) // 2
 
     def one_plane(dz, carry):
         g0 = 2 * (z - dz) + x
-
-        @pl.when((g0 >= 0) & (g0 >= 2 * z - reach))
-        def _():
-            for p in range(2):
+        g1 = 2 * (z - dz + 1) + 1 - x
+        for p in range(hk):
+
+            @pl.when(held(g0))
+            def _(p=p):
                 arrive(g0 * 2 + c, p)
                 forward(g0, True, p)
 
-        across_block(dz - 1)
+            across_piece(g1, p)
 
         @pl.when(need(g0, g))
         def _():
-            sibling(g0)
-            compute(g0)
+            set_mask(g0)
+            for p in range(hk):
+                sibling(g0, p)
+                compute(g0, p)
 
         return carry
 
     lax.fori_loop(1, last + 1, one_plane, 0)
-    across_block(last)
+    for p in range(hk):
+        across_piece(2 * (z - last) + 1 - x, p)
 
     for i in range(hk):
         for j in range(G):
@@ -300,21 +317,24 @@
             o = acc[i, :HD, at] * (1.0 / total) + mean_t[i]
             out_ref[:, (i * G + j) * HD : (i * G + j + 1) * HD] = o.astype(jnp.bfloat16).T
 
-    for one in head_copies:
+    for one in head_copies.values():
         one.wait_send()
+
+    drain(g, True, (hk - 1,), (0, 1))
+    drain(g, True, range(hk), (2,))
 
     def settle(dz, carry):
         g0 = 2 * (z - dz) + x
 
-        @pl.when((dz == 0) | (g0 >= 0) & (g0 >= 2 * z - reach))
+        @pl.when((dz > 0) & held(g0))
         def _():
-            drain(g0, True)
+            drain(g0, True, range(hk))
 
         g1 = 2 * (z - dz) + 1 - x
 
         @pl.when(need(g1, g))
         def _():
-            drain(g1, False)
+            drain(g1, False, range(hk))
 
         return carry
 
@@ -339,7 +359,7 @@
         in_specs=[hbm] * 7,
         out_specs=vmem,
         scratch_shapes=[
-            pltpu.VMEM((nseq, 2 * rows + 16, cols), jnp.bfloat16),
+            pltpu.VMEM((nseq, hk, 2 * rows + 16, HD), jnp.bfloat16),
             pltpu.VMEM((rows, width), jnp.bfloat16),
             pltpu.SMEM(doc_lengths.shape, jnp.int32),
             pltpu.VMEM(key_scales.shape, jnp.bfloat16),
@@ -352,10 +372,11 @@
             pltpu.VMEM((2 * rows, rows), jnp.float32),
             pltpu.VMEM((1, rows), jnp.int32),
             dma((7,)),
-            dma((2, max(nh - 1, 1))),
-            dma((2, max(nh - 1, 1))),
-            dma((3, nseq, 2)),
-            dma((nseq, 2)),
+            dma((2, hk)),
+            dma((2, hk, max(nh - 1, 1))),
+            dma((2, hk, max(nh - 1, 1))),
+            dma((3, nseq, hk)),
+            dma((nseq, hk)),
         ],
         compiler_params=pltpu.CompilerParams(
             collective_id=0, has_side_effects=True, vmem_limit_bytes=62 * 1024 * 1024

time: 41.1 us -> 46.7 us (1.14)
  Pallas kernels: 38.6 us -> 44.2 us
    pallas_call x1, Pallas kernels: 38.6 us -> 44.2 us  [shards(): pl.pallas_call(functools.partial(kernel, dims), out_shape=jax.ShapeDtypeS...]
where the time goes in v3:
time: 46.7 us; the launch traced here: 46.5 us
  Pallas kernels  44.2 us (95%)
  local copies, waits for them, and re-layouts  2.29 us (5%)
    pallas_call x1, Pallas kernels, shards(): pl.pallas_call(functools.partial(kernel, dims), out_shape=jax.ShapeDtypeS...  44.2 us
    unnamed x1, local copies, waits for them, and re-layouts  2.29 us

profile of v3, /device:TPU:25, one launch (start us, length us, event | category | flops | bytes accessed | tf_op | source)
XLA Modules:
  0.0 46.5 jit_solution(14268461475036273094)
XLA Ops:
  0.0 44.2 %attend.1 = bf16[128,4096]{1,0:T(8,128)(2,1)} custom-call(s32[64]{0:T(128)} %doc_hbm.1, bf16[128,4096]{1,0:T(8,128)(2,1)} %q_hbm.1, bf16[64,1024]{1,0:T(8,128)(2,1)} %k_hbm.1, bf16[64,1024]{1,0:T(8,128)(2,1)} %v_hbm.1, bf16[2,4]{1,0:T(2,128)(2,1)} %ks_hbm.1, bf16[2,4]{1,0:T(2,128)(2,1)} %vs_hbm.1, f32[1,512]{1,0:T(1,128)} %bitcast.1), custom_call_target="tpu_custom_call" | custom-call | flops 3221225472 | bytes 2097152 | tf_op jit(solution)/shard_map/attend/pallas_call | solution.py:356
  44.2 2.3 %copy.9 = bf16[128,4096]{1,0:T(8,128)(2,1)} copy(bf16[128,4096]{1,0:T(8,128)(2,1)} %attend.1) | data formatting | bytes 2097152

commit v4 on v3

--- a/solution.py
+++ b/solution.py
@@ -34,10 +34,12 @@
     ks_ref,
     vs_ref,
     mean_ref,
-    qt,
+    qs,
     acc,
     m_ref,
-    mean_t,
+    s_scr,
+    p_scr,
+    f_scr,
     bias,
     lo_ref,
     local_sem,
@@ -48,6 +50,8 @@
     recv,
 ):
     planes, nh, rows, hk, toks, reach = dims
+    pp = math.gcd(hk, 2)
+    np_ = hk // pp
     cols = hk * HD
     s = lax.axis_index("seq")
     h = lax.axis_index("head")
@@ -126,7 +130,7 @@
         buf[s, i, 2 * rows :, :] = jnp.concatenate(scale_rows, axis=0).astype(jnp.bfloat16)
 
     def part(slot, p):
-        return buf.at[slot, p]
+        return buf.at[slot, pl.ds(p * pp, pp)]
 
     def copy(kind, slot, p, dst):
         return pltpu.make_async_remote_copy(
@@ -179,89 +183,83 @@
         copy(2, slot, p, cdst).wait_recv()
 
     def own_piece(i):
-        for piece in range(2):
-            locals_[piece, i].wait()
-            for step in range(1, nh):
-                head_copies[piece, i, step].wait_recv()
+        for j in range(i * pp, (i + 1) * pp):
+            for piece in range(2):
+                locals_[piece, j].wait()
+                for step in range(1, nh):
+                    head_copies[piece, j, step].wait_recv()
         forward(g, True, i)
 
     own_piece(0)
 
     small[2].wait()
     small[3].wait()
-    pos = s * rows + lax.broadcasted_iota(jnp.int32, (1, rows), 1)
+    pos = s * rows + lax.broadcasted_iota(jnp.int32, (rows, 1), 0)
     start = jnp.int32(0)
-    low = jnp.zeros((1, rows), jnp.int32)
+    low = jnp.zeros((rows, 1), jnp.int32)
     for j in range(doc_ref.shape[0]):
         low = jnp.where(pos >= start, start, low)
         start = start + doc_ref[j]
-    lo_ref[...] = low
+    lo_ref[...] = jnp.broadcast_to(low, lo_ref.shape)
     m_ref[...] = jnp.full(m_ref.shape, NEG, jnp.float32)
     acc[...] = jnp.zeros(acc.shape, jnp.float32)
     q_copy.wait()
     for i in range(hk):
         for j in range(G):
-            tile = q_vm[:, (i * G + j) * HD : (i * G + j + 1) * HD]
-            qt[i, :, j * rows : (j + 1) * rows] = tile.T
-        mean_t[i] = jnp.broadcast_to(mean_ref[:, i * HD : (i + 1) * HD], (rows, HD)).T
+            qs[i, j * rows : (j + 1) * rows, :] = q_vm[:, (i * G + j) * HD : (i * G + j + 1) * HD]
 
     keys = 2 * rows
     blocks = keys // BLK
-    wide = 2 * rows
+    lane = lax.broadcasted_iota(jnp.int32, (1, HD), 1)
 
     def set_mask(g0):
-        key_pos = g0 * keys + lax.broadcasted_iota(jnp.int32, (keys, rows), 0)
-        query_pos = s * rows + lax.broadcasted_iota(jnp.int32, (keys, rows), 1)
-        ok = (key_pos >= lo_ref[...]) & (key_pos <= query_pos)
+        key_pos = g0 * keys + lax.broadcasted_iota(jnp.int32, (rows, keys), 1)
+        query_pos = s * rows + lax.broadcasted_iota(jnp.int32, (rows, keys), 0)
+        low = jnp.concatenate([lo_ref[...], lo_ref[...]], axis=1)
+        ok = (key_pos >= low) & (key_pos <= query_pos)
         bias[...] = jnp.where(ok, 0.0, NEG)
 
-    def compute(g0, i):
-        mask = jnp.concatenate([bias[...], bias[...]], axis=1)
-        units = [(i, j) for j in range(G * rows // wide)]
-        lane = lax.broadcasted_iota(jnp.int32, (1, HD), 1)
-        sub = lax.broadcasted_iota(jnp.int32, (16, keys), 0)
-
-        def head_of(i):
+    def compute(g0, p):
+        heads = range(p * pp, (p + 1) * pp)
+
+        def along(sc):
+            return jnp.concatenate(
+                [jnp.where(lane < BLK, sc[n // per, n % per][None], sc[n // per, n % per + 1][None])
+                 for n in range(0, blocks, 2)],
+                axis=1,
+            )
+
+        rows_of, values = {}, {}
+        for i in heads:
             k = buf[pl.ds(2 * g0, 2), i, 0:rows, :].reshape(keys, HD)
+            s_scr[i % pp] = lax.dot_general(
+                qs[i], k, (((1,), (1,)), ((), ())), preferred_element_type=jnp.float32
+            )
             v = buf[pl.ds(2 * g0, 2), i, rows : 2 * rows, :].reshape(keys, HD)
             sc = buf[pl.ds(2 * g0, 2), i, 2 * rows : 2 * rows + 16, :].astype(jnp.float32)
-            ks = sc[:, 0:per].reshape(blocks, 1, HD) * SCALE
-            vs = sc[:, per : 2 * per].reshape(blocks, 1, HD)
-            inv = 1.0 / vs
-            inv = jnp.concatenate(
-                [jnp.where(lane < BLK, inv[2 * n], inv[2 * n + 1]) for n in range(2)], axis=1
-            )
+            vs = sc[:, per : 2 * per]
+            rows_of[i] = (along(sc[:, 0:per] * SCALE), along(jnp.log2(vs)))
+            inv = 1.0 / vs.reshape(blocks, 1, HD)
             high = inv.astype(jnp.bfloat16).astype(jnp.float32)
-            both = jnp.where(sub == 0, high, jnp.where(sub == 1, inv - high, 0.0))
-            vt = jnp.concatenate([v.T, both.astype(jnp.bfloat16)], axis=0)
-            lvs = jnp.log2(vs)
-            ks = jnp.concatenate([ks, ks], axis=2)
-            lvs = jnp.concatenate([lvs, lvs], axis=2)
-            return k, vt, ks, lvs
-
-        def score(unit, head):
-            i, j = unit
-            return jnp.dot(
-                head[0], qt[i, :, j * wide : (j + 1) * wide], preferred_element_type=jnp.float32
-            )
-
-        head = head_of(i)
-        _, vt, ks, lvs = head
-        ahead = score(units[0], head)
-        for n, (i, j) in enumerate(units):
-            raw = ahead
-            if n + 1 < len(units):
-                ahead = score(units[n + 1], head)
-            at = slice(j * wide, (j + 1) * wide)
-            sco = (raw.reshape(blocks, BLK, wide) * ks).reshape(keys, wide) + mask
-            old = m_ref[i, :, at]
-            new = jnp.maximum(old, jnp.max(sco, axis=0, keepdims=True))
-            fac = jnp.exp2(old - new)
-            m_ref[i, :, at] = new
-            w = jnp.exp2(sco.reshape(blocks, BLK, wide) - (new.reshape(1, 1, wide) - lvs))
-            wb = w.reshape(keys, wide).astype(jnp.bfloat16)
-            got = jnp.dot(vt, wb, preferred_element_type=jnp.float32)
-            acc[i, :, at] = acc[i, :, at] * fac + got[: HD + 8]
+            low = inv - high
+            both = jnp.where(lane[None] == 0, high, jnp.where(lane[None] == 1, low, 0.0))
+            both = jnp.broadcast_to(both, (blocks, BLK, HD)).reshape(keys, HD)
+            values[i] = jnp.concatenate([v, both.astype(jnp.bfloat16)], axis=1)
+        for i in heads:
+            ks, lvs = rows_of[i]
+            add = bias[...] + lvs
+            for j in range(G):
+                at = slice(j * rows, (j + 1) * rows)
+                sco = s_scr[i % pp, at, :] * ks + add
+                old = m_ref[i, at, :]
+                new = jnp.maximum(old, jnp.max(sco, axis=1, keepdims=True))
+                m_ref[i, at, :] = new
+                f_scr[i % pp, at, :] = jnp.exp2(old - new)
+                w = jnp.exp2(sco - jnp.concatenate([new, new], axis=1))
+                p_scr[i % pp, at, :] = w.astype(jnp.bfloat16)
+            got = jnp.dot(p_scr[i % pp], values[i], preferred_element_type=jnp.float32)
+            fac = f_scr[i % pp]
+            acc[i] = acc[i] * jnp.concatenate([fac, fac], axis=1) + got
 
     def sibling(g0, p):
         arrive(g0 * 2 + 1 - c, p)
@@ -277,8 +275,8 @@
             compute(g0, p)
 
     set_mask(g)
-    for i in range(hk):
-        if i + 1 < hk:
+    for i in range(np_):
+        if i + 1 < np_:
             drain(g, True, (i,), (0, 1))
             own_piece(i + 1)
         sibling(g, i)
@@ -288,7 +286,7 @@
     def one_plane(dz, carry):
         g0 = 2 * (z - dz) + x
         g1 = 2 * (z - dz + 1) + 1 - x
-        for p in range(hk):
+        for p in range(np_):
 
             @pl.when(held(g0))
             def _(p=p):
@@ -300,41 +298,41 @@
         @pl.when(need(g0, g))
         def _():
             set_mask(g0)
-            for p in range(hk):
+            for p in range(np_):
                 sibling(g0, p)
                 compute(g0, p)
 
         return carry
 
     lax.fori_loop(1, last + 1, one_plane, 0)
-    for p in range(hk):
+    for p in range(np_):
         across_piece(2 * (z - last) + 1 - x, p)
 
     for i in range(hk):
         for j in range(G):
             at = slice(j * rows, (j + 1) * rows)
-            total = acc[i, HD : HD + 1, at] + acc[i, HD + 1 : HD + 2, at]
-            o = acc[i, :HD, at] * (1.0 / total) + mean_t[i]
-            out_ref[:, (i * G + j) * HD : (i * G + j + 1) * HD] = o.astype(jnp.bfloat16).T
+            total = acc[i, at, HD : HD + 1] + acc[i, at, HD + 1 : HD + 2]
+            o = acc[i, at, :HD] * (1.0 / total) + mean_ref[:, i * HD : (i + 1) * HD]
+            out_ref[:, (i * G + j) * HD : (i * G + j + 1) * HD] = o.astype(jnp.bfloat16)
 
     for one in head_copies.values():
         one.wait_send()
 
-    drain(g, True, (hk - 1,), (0, 1))
-    drain(g, True, range(hk), (2,))
+    drain(g, True, (np_ - 1,), (0, 1))
+    drain(g, True, range(np_), (2,))
 
     def settle(dz, carry):
         g0 = 2 * (z - dz) + x
 
         @pl.when((dz > 0) & held(g0))
         def _():
-            drain(g0, True, range(hk))
+            drain(g0, True, range(np_))
 
         g1 = 2 * (z - dz) + 1 - x
 
         @pl.when(need(g1, g))
         def _():
-            drain(g1, False, range(hk))
+            drain(g1, False, range(np_))
 
         return carry
 
@@ -365,12 +363,14 @@
             pltpu.VMEM(key_scales.shape, jnp.bfloat16),
             pltpu.VMEM(value_scales.shape, jnp.bfloat16),
             pltpu.VMEM((1, cols), jnp.float32),
-            pltpu.VMEM((hk, HD, G * rows), jnp.bfloat16),
-            pltpu.VMEM((hk, HD + 8, G * rows), jnp.float32),
-            pltpu.VMEM((hk, 1, G * rows), jnp.float32),
-            pltpu.VMEM((hk, HD, rows), jnp.float32),
-            pltpu.VMEM((2 * rows, rows), jnp.float32),
-            pltpu.VMEM((1, rows), jnp.int32),
+            pltpu.VMEM((hk, G * rows, HD), jnp.bfloat16),
+            pltpu.VMEM((hk, G * rows, 2 * HD), jnp.float32),
+            pltpu.VMEM((hk, G * rows, HD), jnp.float32),
+            pltpu.VMEM((math.gcd(hk, 2), G * rows, 2 * rows), jnp.float32),
+            pltpu.VMEM((math.gcd(hk, 2), G * rows, 2 * rows), jnp.bfloat16),
+            pltpu.VMEM((math.gcd(hk, 2), G * rows, HD), jnp.float32),
+            pltpu.VMEM((rows, 2 * rows), jnp.float32),
+            pltpu.VMEM((rows, HD), jnp.int32),
             dma((7,)),
             dma((2, hk)),
             dma((2, hk, max(nh - 1, 1))),

time: 46.7 us -> 41.8 us (0.90)
  Pallas kernels: 44.2 us -> 39.4 us
    pallas_call x1, Pallas kernels: 44.2 us -> 39.4 us  [shards(): pl.pallas_call(functools.partial(kernel, dims), out_shape=jax.ShapeDtypeS...]
where the time goes in v4:
time: 41.8 us; the launch traced here: 41.7 us
  Pallas kernels  39.4 us (94%)
  local copies, waits for them, and re-layouts  2.29 us (5%)
    pallas_call x1, Pallas kernels, shards(): pl.pallas_call(functools.partial(kernel, dims), out_shape=jax.ShapeDtypeS...  39.4 us
    unnamed x1, local copies, waits for them, and re-layouts  2.29 us

profile of v4, /device:TPU:25, one launch (start us, length us, event | category | flops | bytes accessed | tf_op | source)
XLA Modules:
  0.0 41.7 jit_solution(3420607117747820059)
XLA Ops:
  0.0 39.4 %attend.1 = bf16[128,4096]{1,0:T(8,128)(2,1)} custom-call(s32[64]{0:T(128)} %doc_hbm.1, bf16[128,4096]{1,0:T(8,128)(2,1)} %q_hbm.1, bf16[64,1024]{1,0:T(8,128)(2,1)} %k_hbm.1, bf16[64,1024]{1,0:T(8,128)(2,1)} %v_hbm.1, bf16[2,4]{1,0:T(2,128)(2,1)} %ks_hbm.1, bf16[2,4]{1,0:T(2,128)(2,1)} %vs_hbm.1, f32[1,512]{1,0:T(1,128)} %bitcast.1), custom_call_target="tpu_custom_call" | custom-call | flops 3221225472 | bytes 2097152 | tf_op jit(solution)/shard_map/attend/pallas_call | solution.py:354
  39.4 2.3 %copy.9 = bf16[128,4096]{1,0:T(8,128)(2,1)} copy(bf16[128,4096]{1,0:T(8,128)(2,1)} %attend.1) | data formatting | bytes 2097152

commit v5 on v4

--- a/solution.py
+++ b/solution.py
@@ -37,6 +37,7 @@
     qs,
     acc,
     m_ref,
+    l_ref,
     s_scr,
     p_scr,
     f_scr,
@@ -182,16 +183,6 @@
     def arrive(slot, p):
         copy(2, slot, p, cdst).wait_recv()
 
-    def own_piece(i):
-        for j in range(i * pp, (i + 1) * pp):
-            for piece in range(2):
-                locals_[piece, j].wait()
-                for step in range(1, nh):
-                    head_copies[piece, j, step].wait_recv()
-        forward(g, True, i)
-
-    own_piece(0)
-
     small[2].wait()
     small[3].wait()
     pos = s * rows + lax.broadcasted_iota(jnp.int32, (rows, 1), 0)
@@ -202,11 +193,20 @@
         start = start + doc_ref[j]
     lo_ref[...] = jnp.broadcast_to(low, lo_ref.shape)
     m_ref[...] = jnp.full(m_ref.shape, NEG, jnp.float32)
+    l_ref[...] = jnp.zeros(l_ref.shape, jnp.float32)
     acc[...] = jnp.zeros(acc.shape, jnp.float32)
     q_copy.wait()
     for i in range(hk):
         for j in range(G):
             qs[i, j * rows : (j + 1) * rows, :] = q_vm[:, (i * G + j) * HD : (i * G + j + 1) * HD]
+
+    def own_piece(i):
+        for j in range(i * pp, (i + 1) * pp):
+            for piece in range(2):
+                locals_[piece, j].wait()
+                for step in range(1, nh):
+                    head_copies[piece, j, step].wait_recv()
+        forward(g, True, i)
 
     keys = 2 * rows
     blocks = keys // BLK
@@ -237,29 +237,23 @@
             )
             v = buf[pl.ds(2 * g0, 2), i, rows : 2 * rows, :].reshape(keys, HD)
             sc = buf[pl.ds(2 * g0, 2), i, 2 * rows : 2 * rows + 16, :].astype(jnp.float32)
-            vs = sc[:, per : 2 * per]
-            rows_of[i] = (along(sc[:, 0:per] * SCALE), along(jnp.log2(vs)))
-            inv = 1.0 / vs.reshape(blocks, 1, HD)
-            high = inv.astype(jnp.bfloat16).astype(jnp.float32)
-            low = inv - high
-            both = jnp.where(lane[None] == 0, high, jnp.where(lane[None] == 1, low, 0.0))
-            both = jnp.broadcast_to(both, (blocks, BLK, HD)).reshape(keys, HD)
-            values[i] = jnp.concatenate([v, both.astype(jnp.bfloat16)], axis=1)
+            rows_of[i] = (along(sc[:, 0:per] * SCALE), along(sc[:, per : 2 * per]))
+            values[i] = v
         for i in heads:
-            ks, lvs = rows_of[i]
-            add = bias[...] + lvs
+            ks, vs = rows_of[i]
             for j in range(G):
                 at = slice(j * rows, (j + 1) * rows)
-                sco = s_scr[i % pp, at, :] * ks + add
+                sco = s_scr[i % pp, at, :] * ks + bias[...]
                 old = m_ref[i, at, :]
                 new = jnp.maximum(old, jnp.max(sco, axis=1, keepdims=True))
                 m_ref[i, at, :] = new
-                f_scr[i % pp, at, :] = jnp.exp2(old - new)
+                fac = jnp.exp2(old - new)
+                f_scr[i % pp, at, :] = fac
                 w = jnp.exp2(sco - jnp.concatenate([new, new], axis=1))
-                p_scr[i % pp, at, :] = w.astype(jnp.bfloat16)
+                l_ref[i, at, :] = l_ref[i, at, :] * fac + (w[:, :HD] + w[:, HD:])
+                p_scr[i % pp, at, :] = (w * vs).astype(jnp.bfloat16)
             got = jnp.dot(p_scr[i % pp], values[i], preferred_element_type=jnp.float32)
-            fac = f_scr[i % pp]
-            acc[i] = acc[i] * jnp.concatenate([fac, fac], axis=1) + got
+            acc[i] = acc[i] * f_scr[i % pp] + got
 
     def sibling(g0, p):
         arrive(g0 * 2 + 1 - c, p)
@@ -276,9 +270,9 @@
 
     set_mask(g)
     for i in range(np_):
-        if i + 1 < np_:
-            drain(g, True, (i,), (0, 1))
-            own_piece(i + 1)
+        if i > 0:
+            drain(g, True, (i - 1,), (0, 1))
+        own_piece(i)
         sibling(g, i)
         compute(g, i)
     last = (reach + 1) // 2
@@ -311,8 +305,8 @@
     for i in range(hk):
         for j in range(G):
             at = slice(j * rows, (j + 1) * rows)
-            total = acc[i, at, HD : HD + 1] + acc[i, at, HD + 1 : HD + 2]
-            o = acc[i, at, :HD] * (1.0 / total) + mean_ref[:, i * HD : (i + 1) * HD]
+            total = jnp.sum(l_ref[i, at, :], axis=1, keepdims=True)
+            o = acc[i, at, :] * (1.0 / total) + mean_ref[:, i * HD : (i + 1) * HD]
             out_ref[:, (i * G + j) * HD : (i * G + j + 1) * HD] = o.astype(jnp.bfloat16)
 
     for one in head_copies.values():
@@ -364,7 +358,8 @@
             pltpu.VMEM(value_scales.shape, jnp.bfloat16),
             pltpu.VMEM((1, cols), jnp.float32),
             pltpu.VMEM((hk, G * rows, HD), jnp.bfloat16),
-            pltpu.VMEM((hk, G * rows, 2 * HD), jnp.float32),
+            pltpu.VMEM((hk, G * rows, HD), jnp.float32),
+            pltpu.VMEM((hk, G * rows, HD), jnp.float32),
             pltpu.VMEM((hk, G * rows, HD), jnp.float32),
             pltpu.VMEM((math.gcd(hk, 2), G * rows, 2 * rows), jnp.float32),
             pltpu.VMEM((math.gcd(hk, 2), G * rows, 2 * rows), jnp.bfloat16),

time: 41.8 us -> 39.6 us (0.947)
  Pallas kernels: 39.4 us -> 37.2 us
    pallas_call x1, Pallas kernels: 39.4 us -> 37.2 us  [shards(): pl.pallas_call(functools.partial(kernel, dims), out_shape=jax.ShapeDtypeS...]
where the time goes in v5:
time: 39.6 us; the launch traced here: 39.5 us
  Pallas kernels  37.2 us (94%)
  local copies, waits for them, and re-layouts  2.29 us (6%)
    pallas_call x1, Pallas kernels, shards(): pl.pallas_call(functools.partial(kernel, dims), out_shape=jax.ShapeDtypeS...  37.2 us
    unnamed x1, local copies, waits for them, and re-layouts  2.29 us

profile of v5, /device:TPU:25, one launch (start us, length us, event | category | flops | bytes accessed | tf_op | source)
XLA Modules:
  0.0 39.5 jit_solution(14137894598351606190)
XLA Ops:
  0.0 37.2 %attend.1 = bf16[128,4096]{1,0:T(8,128)(2,1)} custom-call(s32[64]{0:T(128)} %doc_hbm.1, bf16[128,4096]{1,0:T(8,128)(2,1)} %q_hbm.1, bf16[64,1024]{1,0:T(8,128)(2,1)} %k_hbm.1, bf16[64,1024]{1,0:T(8,128)(2,1)} %v_hbm.1, bf16[2,4]{1,0:T(2,128)(2,1)} %ks_hbm.1, bf16[2,4]{1,0:T(2,128)(2,1)} %vs_hbm.1, f32[1,512]{1,0:T(1,128)} %bitcast.1), custom_call_target="tpu_custom_call" | custom-call | flops 3221225472 | bytes 2097152 | tf_op jit(solution)/shard_map/attend/pallas_call | solution.py:348
  37.2 2.3 %copy.9 = bf16[128,4096]{1,0:T(8,128)(2,1)} copy(bf16[128,4096]{1,0:T(8,128)(2,1)} %attend.1) | data formatting | bytes 2097152

commit v6 on v5

--- a/solution.py
+++ b/solution.py
@@ -27,7 +27,7 @@
     ks_hbm,
     vs_hbm,
     mean_hbm,
-    out_ref,
+    out_hbm,
     buf,
     q_vm,
     doc_ref,
@@ -41,9 +41,11 @@
     s_scr,
     p_scr,
     f_scr,
+    out_vm,
     bias,
     lo_ref,
     local_sem,
+    out_sem,
     own_sem,
     head_send,
     head_recv,
@@ -106,20 +108,24 @@
     )
 
     head_copies = {}
-    for i in range(hk):
-        for piece, hbm in enumerate((k_hbm, v_hbm)):
-            for step in range(1, nh):
-                peer = (h + step) % nh
-                one = pltpu.make_async_remote_copy(
-                    src_ref=hbm.at[:, columns(peer, i)],
-                    dst_ref=own_part(piece, i),
-                    send_sem=head_send.at[piece, i, step - 1],
-                    recv_sem=head_recv.at[piece, i, step - 1],
-                    device_id=(s, peer),
-                    device_id_type=MESH,
-                )
-                head_copies[piece, i, step] = one
-                one.start()
+
+    def exchange(heads):
+        for i in heads:
+            for piece, hbm in enumerate((k_hbm, v_hbm)):
+                for step in range(1, nh):
+                    peer = (h + step) % nh
+                    one = pltpu.make_async_remote_copy(
+                        src_ref=hbm.at[:, columns(peer, i)],
+                        dst_ref=own_part(piece, i),
+                        send_sem=head_send.at[piece, i, step - 1],
+                        recv_sem=head_recv.at[piece, i, step - 1],
+                        device_id=(s, peer),
+                        device_id_type=MESH,
+                    )
+                    head_copies[piece, i, step] = one
+                    one.start()
+
+    exchange(range(pp))
 
     per = rows // BLK
     small[0].wait()
@@ -199,6 +205,8 @@
     for i in range(hk):
         for j in range(G):
             qs[i, j * rows : (j + 1) * rows, :] = q_vm[:, (i * G + j) * HD : (i * G + j + 1) * HD]
+
+    exchange(range(pp, hk))
 
     def own_piece(i):
         for j in range(i * pp, (i + 1) * pp):
@@ -299,15 +307,20 @@
         return carry
 
     lax.fori_loop(1, last + 1, one_plane, 0)
+    outs = []
     for p in range(np_):
         across_piece(2 * (z - last) + 1 - x, p)
-
-    for i in range(hk):
-        for j in range(G):
-            at = slice(j * rows, (j + 1) * rows)
-            total = jnp.sum(l_ref[i, at, :], axis=1, keepdims=True)
-            o = acc[i, at, :] * (1.0 / total) + mean_ref[:, i * HD : (i + 1) * HD]
-            out_ref[:, (i * G + j) * HD : (i * G + j + 1) * HD] = o.astype(jnp.bfloat16)
+        for i in range(p * pp, (p + 1) * pp):
+            for j in range(G):
+                at = slice(j * rows, (j + 1) * rows)
+                total = jnp.sum(l_ref[i, at, :], axis=1, keepdims=True)
+                o = acc[i, at, :] * (1.0 / total) + mean_ref[:, i * HD : (i + 1) * HD]
+                out_vm[:, (i * G + j) * HD : (i * G + j + 1) * HD] = o.astype(jnp.bfloat16)
+            span = pl.ds(i * G * HD, G * HD)
+            outs.append(
+                pltpu.make_async_copy(out_vm.at[:, span], out_hbm.at[:, span], out_sem.at[i])
+            )
+            outs[-1].start()
 
     for one in head_copies.values():
         one.wait_send()
@@ -331,6 +344,8 @@
         return carry
 
     lax.fori_loop(0, last + 1, settle, 0)
+    for one in outs:
+        one.wait()
 
 
 def shards(queries, key_tokens, value_tokens, key_scales, value_scales, value_means, doc_lengths, nseq, nh):
@@ -343,13 +358,12 @@
     reach = (window + 1) // 2
     dims = (nseq // 4, nh, rows, hk, toks, reach)
     hbm = pl.BlockSpec(memory_space=pltpu.HBM)
-    vmem = pl.BlockSpec(memory_space=pltpu.VMEM)
     dma = pltpu.SemaphoreType.DMA
     return pl.pallas_call(
         functools.partial(kernel, dims),
         out_shape=jax.ShapeDtypeStruct((rows, width), jnp.bfloat16),
         in_specs=[hbm] * 7,
-        out_specs=vmem,
+        out_specs=pl.BlockSpec(memory_space=pl.ANY),
         scratch_shapes=[
             pltpu.VMEM((nseq, hk, 2 * rows + 16, HD), jnp.bfloat16),
             pltpu.VMEM((rows, width), jnp.bfloat16),
@@ -364,9 +378,11 @@
             pltpu.VMEM((math.gcd(hk, 2), G * rows, 2 * rows), jnp.float32),
             pltpu.VMEM((math.gcd(hk, 2), G * rows, 2 * rows), jnp.bfloat16),
             pltpu.VMEM((math.gcd(hk, 2), G * rows, HD), jnp.float32),
+            pltpu.VMEM((rows, width), jnp.bfloat16),
             pltpu.VMEM((rows, 2 * rows), jnp.float32),
             pltpu.VMEM((rows, HD), jnp.int32),
             dma((7,)),
+            dma((hk,)),
             dma((2, hk)),
             dma((2, hk, max(nh - 1, 1))),
             dma((2, hk, max(nh - 1, 1))),

time: 39.6 us -> 39.5 us (level)
  no operation moved by 1% of the time
where the time goes in v6:
time: 39.5 us; the launch traced here: 39.4 us
  Pallas kernels  37.1 us (94%)
  local copies, waits for them, and re-layouts  2.29 us (6%)
    pallas_call x1, Pallas kernels, shards(): pl.pallas_call(functools.partial(kernel, dims), out_shape=jax.ShapeDtypeS...  37.1 us
    unnamed x1, local copies, waits for them, and re-layouts  2.29 us

profile of v6, /device:TPU:25, one launch (start us, length us, event | category | flops | bytes accessed | tf_op | source)
XLA Modules:
  0.0 39.4 jit_solution(6176037576663439756)
XLA Ops:
  0.0 37.1 %attend.1 = bf16[128,4096]{1,0:T(8,128)(2,1)} custom-call(s32[64]{0:T(128)} %doc_hbm.1, bf16[128,4096]{1,0:T(8,128)(2,1)} %q_hbm.1, bf16[64,1024]{1,0:T(8,128)(2,1)} %k_hbm.1, bf16[64,1024]{1,0:T(8,128)(2,1)} %v_hbm.1, bf16[2,4]{1,0:T(2,128)(2,1)} %ks_hbm.1, bf16[2,4]{1,0:T(2,128)(2,1)} %vs_hbm.1, f32[1,512]{1,0:T(1,128)} %bitcast.1), custom_call_target="tpu_custom_call" | custom-call | flops 3221225472 | bytes 2097152 | tf_op jit(solution)/shard_map/attend/pallas_call | solution.py:362
  37.1 2.3 %copy.9 = bf16[128,4096]{1,0:T(8,128)(2,1)} copy(bf16[128,4096]{1,0:T(8,128)(2,1)} %attend.1) | data formatting | bytes 2097152
